TPU v7x, 256 devices: a whole 4x4x8 slice. The times are simulated.
256 devices in a mesh: head: 8 (over x, y_hi), tok: 32 (over y_lo, z, core).
Axes of the slice: x: 4, y: 4 (y_hi: 2, y_lo: 2; y = y_hi * 2 + y_lo), z: 8, core: 2. Of those that a mesh axis runs over, the one named last changes fastest.
Arguments:
- anchors: bfloat16 [4096, 1024], P('tok'), may hold values from -26 to 26
- cells: bfloat16 [16384, 1024], P('tok'), may hold values from -26 to 26
- w_query: bfloat16 [1024, 1024], P(None, 'head'), may hold values from -0.125 to 0.125
- w_key: bfloat16 [1024, 1024], P(None, 'head'), may hold values from -0.15625 to 0.15625
- w_value: bfloat16 [1024, 1024], P(None, 'head'), may hold values from -0.1875 to 0.1875
- w_out: bfloat16 [1024, 1024], P('head'), may hold values from -0.1875 to 0.1875
- grad_out_anchors: bfloat16 [4096, 1024], P('tok'), may hold values from -96 to 96
- grad_out_cells: bfloat16 [16384, 1024], P('tok'), may hold values from -96 to 96
Outputs:
- grad_anchors: bfloat16 [4096, 1024], P('tok', 'head')
- grad_cells: bfloat16 [16384, 1024], P('tok', 'head')
All inputs are finite; a program needn't handle non-finite values.
Results may differ from a plain program's by a relative error of at most 0.035.
Values may be sent and summed in bfloat16 or wider, within the bound.
No kernel may reach another device: no remote copies, remote signals or barrier semaphores. Data moves between devices by JAX's collectives and lax.ppermute only.
A program may use at most 64 MiB of HBM per device.

v0:
```python
import functools

import jax
import jax.numpy as jnp
from jax import lax
from jax.experimental import pallas as pl
from jax.experimental.pallas import tpu as pltpu
from jax.sharding import PartitionSpec as P

HEAD_DIM = 64
SCALE = HEAD_DIM ** (-0.5)
LOG2E = 1.4426950408889634
Y_LO, Z, CORES = 2, 8, 2
X, Y_HI = 4, 2
HEAD = ("x", "y_hi")
TOK = ("y_lo", "z", "core")
STEP = 128
BF16 = jnp.bfloat16
F32 = jnp.float32
COST = {"scores": 15 * 10**8, "pair": 15 * 10**8, "anchors": 10**8}


def tok_perm(move):
    pairs = []
    for yl in range(Y_LO):
        for z in range(Z):
            for core in range(CORES):
                yl2, z2, core2 = move(yl, z, core)
                pairs.append(
                    ((yl * Z + z) * CORES + core, (yl2 * Z + z2 % Z) * CORES + core2)
                )
    return pairs


def head_perm(move):
    pairs = []
    for x in range(X):
        for yh in range(Y_HI):
            x2, yh2 = move(x, yh)
            pairs.append((x * Y_HI + yh, (x2 % X) * Y_HI + yh2))
    return pairs


SWAP_CORE = tok_perm(lambda yl, z, c: (yl, z, 1 - c))
SWAP_Y = tok_perm(lambda yl, z, c: (1 - yl, z, c))
SWAP_BOTH = tok_perm(lambda yl, z, c: (1 - yl, z, 1 - c))
GATHER = [
    tok_perm(lambda yl, z, c: (yl, z, 0) if c == 0 else (yl, z - 1, 1)),
    tok_perm(lambda yl, z, c: (yl, z - 1, 1) if c == 0 else (yl, z, 0)),
]
RETURN = [[(b, a) for a, b in perm] for perm in GATHER]
HOPS = 3
FORTH = [
    tok_perm(lambda yl, z, c, j=j: (yl, z + j, 0) if c == 0 else (yl, z - j, 1))
    for j in range(HOPS + 1)
]
BACK = [[(b, a) for a, b in perm] for perm in FORTH]
SHIFT_X = [head_perm(lambda x, yh, r=r: (x + r, yh)) for r in range(X)]
SWAP_YH = head_perm(lambda x, yh: (x, 1 - yh))


def dot(a, b, ca, cb):
    return lax.dot_general(a, b, (((ca,), (cb,)), ((), ())), preferred_element_type=F32)


def call(body, outs, args, name, scratch=(), smem=0, hbm=(), after=(), vmem=20):
    def spec(i):
        if i < smem:
            return pl.BlockSpec(memory_space=pltpu.SMEM)
        if i >= len(args):
            return pl.BlockSpec(memory_space=pl.ANY)
        return pl.BlockSpec(memory_space=pltpu.HBM if i in hbm else pltpu.VMEM)

    def kernel(*refs):
        body(*refs[: len(args)], *refs[len(args) + len(after) :])

    return pl.pallas_call(
        kernel,
        out_shape=tuple(outs),
        in_specs=[spec(i) for i in range(len(args) + len(after))],
        out_specs=tuple(pl.BlockSpec(memory_space=pltpu.VMEM) for _ in outs),
        scratch_shapes=list(scratch),
        compiler_params=pltpu.CompilerParams(vmem_limit_bytes=vmem << 20),
        cost_estimate=pl.CostEstimate(
            flops=COST.get(name, 10**10), bytes_accessed=10**6, transcendentals=0
        ),
        name=name,
    )(*args, *after)


def sds(shape, dtype):
    return jax.ShapeDtypeStruct(shape, dtype)


def kv_kernel(rows_hbm, w_key_hbm, w_value_hbm, out, rows, w_key, w_value, sems):
    copies = [
        pltpu.make_async_copy(src, dst, sems.at[i])
        for i, (src, dst) in enumerate(
            ((rows_hbm, rows), (w_key_hbm, w_key), (w_value_hbm, w_value))
        )
    ]
    for copy in copies:
        copy.start()
    copies[0].wait()
    copies[1].wait()
    out[:, 0:128] = dot(rows[...], w_key[...], 1, 0).astype(BF16)
    copies[2].wait()
    out[:, 128:256] = dot(rows[...], w_value[...], 1, 0).astype(BF16)


def qd_kernel(anchors, cells, grad_a, grad_c, w_query, w_out, out):
    na = anchors.shape[0]
    wq = w_query[...]
    wo = w_out[...]
    for lo, rows, grads in ((0, anchors, grad_a), (na, cells, grad_c)):
        hi = lo + rows.shape[0]
        out[lo:hi, 0:128] = dot(rows[...], wq, 1, 0).astype(BF16) * SCALE
        out[lo:hi, 128:256] = dot(grads[...], wo, 1, 1).astype(BF16)


def stats_block(kv, rhs, before, out):
    total = rhs.shape[0] // 2
    keys = kv[:, 0:128]
    values = kv[:, 128:256]

    @pl.loop(0, total // 256)
    def _(index):
        tile = pl.multiple_of(index * 256, 256)
        cols = pl.ds(tile, 256)
        for h in range(2):
            rows = pl.ds(pl.multiple_of(h * total + tile, 256), 256)
            s = dot(keys, rhs[rows, 0:128], 1, 1)
            peak = jnp.max(s, axis=0, keepdims=True) * LOG2E
            if before is not None:
                old_peak = before[h : h + 1, cols]
                peak = jnp.maximum(peak, old_peak)
            e = jnp.exp2(s * LOG2E - peak)
            dp = dot(values, rhs[rows, 128:256], 1, 1)
            norm = jnp.sum(e, axis=0, keepdims=True)
            mass = jnp.sum(e * dp, axis=0, keepdims=True)
            if before is not None:
                factor = jnp.exp2(old_peak - peak)
                norm += factor * before[2 + h : 3 + h, cols]
                mass += factor * before[4 + h : 5 + h, cols]
            out[h : h + 1, cols] = peak
            out[2 + h : 3 + h, cols] = norm
            out[4 + h : 5 + h, cols] = mass

    out[6:8, :] = jnp.zeros((2, total), F32)


def first_stats_kernel(count, *refs):
    first, second = refs[:2]
    blocks = refs[2 : 2 + count]
    stats, rhs = refs[2 + count :]
    half = first.shape[0]
    lane = lax.broadcasted_iota(jnp.int32, (1, 256), 1)
    for h in range(2):
        keep = lane // HEAD_DIM % 2 == h
        for part, rows in enumerate((first, second)):
            x = rows[...]
            lo = (2 * h + part) * half
            rhs[lo : lo + half, :] = jnp.where(keep, x, jnp.zeros_like(x))
    for i, kv in enumerate(blocks):
        stats_block(kv, rhs, stats if i else None, stats)


def first_stats(first, second, blocks):
    total = 2 * first.shape[0]
    return call(
        functools.partial(first_stats_kernel, len(blocks)),
        [sds((8, total), F32), sds((2 * total, 256), BF16)],
        [first, second, *blocks],
        "first_stats",
    )


def next_stats_kernel(kv, rhs, before, stats):
    stats_block(kv, rhs, before, stats)


def both_stats_kernel(kv, rhs_a, rhs_b, before_a, before_b, stats):
    stats_block(kv, rhs_a, before_a, stats.at[0:8])
    stats_block(kv, rhs_b, before_b, stats.at[8:16])


def merged(mine, theirs, a, b, i, j):
    for h in range(2):
        m1 = mine[i + h : i + h + 1, a]
        m2 = theirs[j + h : j + h + 1, b]
        peak = jnp.maximum(m1, m2)
        f1 = jnp.exp2(m1 - peak)
        f2 = jnp.exp2(m2 - peak)
        norm = f1 * mine[i + 2 + h : i + 3 + h, a] + f2 * theirs[j + 2 + h : j + 3 + h, b]
        mass = f1 * mine[i + 4 + h : i + 5 + h, a] + f2 * theirs[j + 4 + h : j + 5 + h, b]
        yield h, peak, norm, mass


def merge_cores_kernel(mine, theirs, out):
    half = mine.shape[1] // 2
    low, high = slice(0, half), slice(half, 2 * half)
    for i in (0, 8):
        for a, b in ((low, high), (high, low)):
            for h, peak, norm, mass in merged(mine, theirs, a, b, i, i):
                out[i + h : i + h + 1, a] = peak
                out[i + 2 + h : i + 3 + h, a] = norm
                out[i + 4 + h : i + 5 + h, a] = mass
        out[i + 6 : i + 8, :] = jnp.zeros((2, 2 * half), F32)


def merge_y_kernel(mine, theirs, out):
    whole = slice(0, mine.shape[1])
    for i, j in ((0, 8), (8, 0)):
        for h, peak, norm, mass in merged(mine, theirs, whole, whole, i, j):
            out[i + h : i + h + 1, whole] = peak + jnp.log(norm) * LOG2E
            out[i + 2 + h : i + 3 + h, whole] = mass / norm
        out[i + 4 : i + 8, :] = jnp.zeros((4, mine.shape[1]), F32)


def scores_kernel(has_before, is_last, *refs):
    first, second, *rhs = refs[:4]
    stats = refs[4]
    refs = refs[5:]
    before = None
    if has_before:
        before, refs = refs[0], refs[1:]
    p_t, ds_t, *dq, kv, keys_t = refs
    kv[: first.shape[0], :] = first[...]
    kv[first.shape[0] :, :] = second[...]
    total = rhs[0].shape[0] // 2
    half = total // 2
    n = kv.shape[0]
    keys_t[...] = kv[:, 0:128].T

    @pl.loop(0, 2)
    def _(h):
        here = pl.ds(pl.multiple_of(h * total, 128), total)
        out = pl.ds(pl.multiple_of(h * HEAD_DIM, HEAD_DIM), HEAD_DIM)
        for g in range(2):
            there = pl.ds(pl.multiple_of((2 * g + h) * total, 128), total)
            lse = stats[pl.ds(8 * g + h, 1), :]
            delta = stats[pl.ds(8 * g + 2 + h, 1), :]
            for c in range(0, n, STEP):
                s = dot(kv[c : c + STEP, 0:128], rhs[g][here, 0:128], 1, 1)
                p = jnp.exp2(s * LOG2E - lse)
                dp = dot(kv[c : c + STEP, 128:256], rhs[g][here, 128:256], 1, 1)
                ds = p * (dp - delta)
                p_t[c : c + STEP, there] = p.astype(BF16)
                ds_t[c : c + STEP, there] = ds.astype(BF16)
            cols = slice(g * total, (g + 1) * total)
            part = dot(keys_t[out, :], ds_t[:, there], 1, 0)
            if has_before:
                part += before[out, cols]
            if is_last:
                dq[2 * g][out, :] = part[:, :half].astype(dq[2 * g].dtype)
                dq[2 * g + 1][out, :] = part[:, half:].astype(BF16)
            else:
                dq[0][out, cols] = part


def scores(blocks, rhs, stats, before, is_last, after=()):
    total = rhs[0].shape[0] // 2
    n = sum(block.shape[0] for block in blocks)
    args = [*blocks, *rhs, stats] + ([] if before is None else [before])
    outs = [sds((n, 4 * total), BF16)] * 2
    if is_last:
        outs += [sds((128, total // 2), F32)] + [sds((128, total // 2), BF16)] * 3
    else:
        outs += [sds((128, 2 * total), F32)]
    return call(
        functools.partial(scores_kernel, before is not None, is_last),
        outs,
        args,
        "scores",
        scratch=[pltpu.VMEM((n, 256), BF16), pltpu.VMEM((128, n), BF16)],
        after=after,
    )


def pair_kernel(first, p_t, ds_t, rhs_a, rhs_b, *outs):
    n = rhs_a.shape[0]
    rows = slice(first, first + sum(out.shape[0] for out in outs))
    for cols, weights in ((slice(0, 128), ds_t), (slice(128, 256), p_t)):
        total = dot(weights[rows, :n], rhs_a[:, cols], 1, 0)
        total += dot(weights[rows, n:], rhs_b[:, cols], 1, 0)
        lo = 0
        for out in outs:
            out[:, cols] = total[lo : lo + out.shape[0]].astype(out.dtype)
            lo += out.shape[0]


def pair(weights, rhs, first, outs, after=()):
    return call(
        functools.partial(pair_kernel, first), outs, [*weights, *rhs], "pair", after=after
    )


def pair_sum_kernel(own, a, b, c, *outs):
    n = outs[0].shape[0]
    for i, out in enumerate(outs):
        rows = slice(i * n, (i + 1) * n)
        more = (a[rows, :].astype(F32) + b[rows, :].astype(F32)) + c[rows, :].astype(F32)
        out[...] = (own[rows, :] + more).astype(BF16)


def weights_kernel(distances, place, w_query, w_key, w_value, *outs):
    width = outs[0].shape[0]
    for r, out in zip(distances, outs):
        lo = pl.multiple_of(lax.rem(place[0] + r, X) * width, width)
        for i, w in enumerate((w_query, w_key, w_value)):
            out[:, i * 128 : (i + 1) * 128] = w[pl.ds(lo, width), :]


def stack_kernel(place, *refs):
    *parts, out = refs
    for side in range(2):
        y_hi = place[1] if side == 0 else 1 - place[1]
        rows = pl.ds(pl.multiple_of(y_hi * 128, 128), 128)
        here = slice(side * 128, (side + 1) * 128)
        for r, part in enumerate(parts):
            out[here, r * 128 : (r + 1) * 128] = part[rows, 0:128]
            lo = (X + 2 * r) * 128
            out[here, lo : lo + 256] = part[rows, 128:384]


def dq_sum_kernel(mine, a, b, c, dq, first):
    more = (a[...].astype(F32) + b[...].astype(F32)) + c[...].astype(F32)
    total = ((mine[...] + more) * SCALE).astype(BF16)
    dq[...] = total
    first[...] = total[:, : first.shape[1]]


def piece_sum_kernel(a, b, out):
    out[...] = (a[...].astype(F32) + b[...].astype(F32)).astype(BF16)


def cells_kernel(own, back_1, back_2a, back_2b, back_3, weights, mine, theirs, dq):
    na = own.shape[1] - mine.shape[0]
    cut = back_2a.shape[1]
    for r, part in ((0, own), (1, back_1), (3, back_3)):
        dq[r * 128 : (r + 1) * 128, :] = part[:, na:]
    dq[256:384, : cut - na] = back_2a[:, na:]
    dq[256:384, cut - na :] = back_2b[...]
    out = dot(dq[...], weights[:, : X * 128], 0, 1)
    mine[...] = out[:, 0:128]
    theirs[...] = out[:, 128:256].astype(BF16)


def anchors_kernel(*refs):
    dqs, dkvs, (weights, cells_mine, cells_theirs, mine, theirs, rows) = refs[:X], refs[X : 2 * X], refs[2 * X :]
    na = rows.shape[0]
    for r, (dq, dkv) in enumerate(zip(dqs, dkvs)):
        rows[:, r * 128 : (r + 1) * 128] = dq[:, :na].T
        lo = X * 128 + r * 256
        rows[:, lo : lo + 256] = dkv[...]
    out = dot(rows[...], weights[...], 1, 1)
    mine[:na, :] = out[:, 0:128]
    theirs[:na, :] = out[:, 128:256].astype(BF16)
    mine[na:, :] = cells_mine[...]
    theirs[na:, :] = cells_theirs[...]


def last_sum_kernel(mine, theirs, anchors, cells):
    na = anchors.shape[0]
    total = (mine[...] + theirs[...].astype(F32)).astype(BF16)
    anchors[...] = total[:na, :]
    cells[...] = total[na:, :]


def over_x(array):
    return [array] + [lax.ppermute(array, HEAD, SHIFT_X[r]) for r in range(1, X)]


def per_device(anchors, cells, w_query, w_key, w_value, w_out, grad_a, grad_c):
    na, nc, d = anchors.shape[0], cells.shape[0], anchors.shape[1]
    rows = na + nc
    total = 2 * rows
    place = jnp.stack([lax.axis_index("x"), lax.axis_index("y_hi")]).astype(jnp.int32)

    (kv,) = call(
        kv_kernel,
        [sds((na, 256), BF16)],
        [anchors, w_key, w_value],
        "kv",
        scratch=[
            pltpu.VMEM((na, d), BF16),
            pltpu.VMEM((d, 128), BF16),
            pltpu.VMEM((d, 128), BF16),
            pltpu.SemaphoreType.DMA((3,)),
        ],
        hbm=(0, 1, 2),
        vmem=60,
    )
    block = jnp.concatenate([lax.ppermute(kv, TOK, perm) for perm in GATHER], axis=0)
    blocks = [block] + [lax.ppermute(block, TOK, FORTH[j]) for j in range(1, HOPS + 1)]

    (mine,) = call(
        qd_kernel,
        [sds((rows, 256), BF16)],
        [anchors, cells, grad_a, grad_c, w_query, w_out],
        "qd",
        after=[place, kv],
    )
    core_rows = lax.ppermute(mine, TOK, SWAP_CORE)
    y_rows = lax.ppermute(mine, TOK, SWAP_Y)
    both_rows = lax.ppermute(y_rows, TOK, SWAP_CORE)

    stats_a, rhs_a = first_stats(mine, core_rows, blocks[:1])
    def weight_rows(distances, after):
        return call(
            functools.partial(weights_kernel, distances),
            [sds((d // X, 3 * 128), BF16)] * len(distances),
            [place, w_query, w_key, w_value],
            "weights",
            smem=1,
            after=after,
        )

    for j in range(1, HOPS):
        (stats_a,) = call(
            next_stats_kernel, [sds((8, total), F32)], [blocks[j], rhs_a, stats_a], "stats"
        )
    stats_b, rhs_b = first_stats(y_rows, both_rows, blocks[:HOPS])
    (stats,) = call(
        both_stats_kernel,
        [sds((16, total), F32)],
        [blocks[HOPS], rhs_a, rhs_b, stats_a, stats_b],
        "both_stats",
    )
    x_weights = weight_rows(tuple(range(X)), [stats])
    x_weights = [x_weights[0]] + [
        lax.ppermute(x_weights[r], HEAD, SHIFT_X[r]) for r in range(1, X)
    ]
    for merge_kernel, perm in ((merge_cores_kernel, SWAP_CORE), (merge_y_kernel, SWAP_Y)):
        (stats,) = call(
            merge_kernel,
            [sds((16, total), F32)],
            [stats, lax.ppermute(stats, TOK, perm)],
            "merge",
        )
    rhs = (rhs_a, rhs_b)
    n = block.shape[0]

    *weights, dq = scores(blocks[3:1:-1], rhs, stats, None, False)
    dkv_3, dkv_2 = pair(weights, rhs, 0, [sds((n, 256), BF16)] * 2)
    sums = [lax.ppermute(dkv_3, TOK, BACK[3]), lax.ppermute(dkv_2, TOK, BACK[2])]
    *weights, dq_mine, dq_core, dq_y, dq_both = scores(
        blocks[1::-1], rhs, stats, dq, True, after=[dkv_3, *x_weights[1:]]
    )
    dq_others = [
        lax.ppermute(part, TOK, perm)
        for part, perm in ((dq_y, SWAP_Y), (dq_both, SWAP_BOTH), (dq_core, SWAP_CORE))
    ]
    (dkv_1,) = pair(weights, rhs, 0, [sds((n, 256), BF16)], after=list(sums))
    sums.append(lax.ppermute(dkv_1, TOK, BACK[1]))
    (dkv,) = pair(weights, rhs, n, [sds((n, 256), F32)], after=[dkv_1])
    pieces = call(
        pair_sum_kernel, [sds((na, 256), BF16)] * len(RETURN), [dkv, *sums], "pair_sum"
    )
    pieces = [lax.ppermute(piece, TOK, perm) for piece, perm in zip(pieces, RETURN)]
    cut = 2 * 128
    dq, dq_first = call(
        dq_sum_kernel,
        [sds((128, rows), BF16), sds((128, cut), BF16)],
        [dq_mine, *dq_others],
        "dq_sum",
        after=[dkv],
    )
    (x_weights,) = call(
        stack_kernel,
        [sds((256, X * 384), BF16)],
        [place, *x_weights],
        "stack",
        smem=1,
        after=[dq],
    )
    back_1 = lax.ppermute(dq, HEAD, SHIFT_X[1])
    back_3 = lax.ppermute(dq, HEAD, SHIFT_X[3])
    back_2a = lax.ppermute(dq_first, HEAD, SHIFT_X[2])
    back_2b = lax.ppermute(back_3[:, cut:], HEAD, SHIFT_X[3])
    cells_mine, cells_theirs = call(
        cells_kernel,
        [sds((nc, 128), F32), sds((nc, 128), BF16)],
        [dq, back_1, back_2a, back_2b, back_3, x_weights],
        "cells",
        scratch=[pltpu.VMEM((X * 128, nc), BF16)],
    )
    (dkv,) = call(
        piece_sum_kernel, [sds((na, 256), BF16)], pieces, "piece_sum", after=[x_weights]
    )
    mine, theirs = call(
        anchors_kernel,
        [sds((rows, 128), F32), sds((rows, 128), BF16)],
        [dq, back_1, back_2a, back_3, *over_x(dkv), x_weights, cells_mine, cells_theirs],
        "anchors",
        scratch=[pltpu.VMEM((na, X * 384), BF16)],
    )
    return call(
        last_sum_kernel,
        [sds((na, 128), BF16), sds((nc, 128), BF16)],
        [mine, lax.ppermute(theirs, HEAD, SWAP_YH)],
        "last_sum",
    )


def solution(mesh):
    parts = jax.sharding.Mesh(mesh.devices.reshape(X, Y_HI, Y_LO, Z, CORES), (*HEAD, *TOK))
    return jax.shard_map(
        per_device,
        mesh=parts,
        in_specs=(
            P(TOK, None),
            P(TOK, None),
            P(None, HEAD),
            P(None, HEAD),
            P(None, HEAD),
            P(HEAD, None),
            P(TOK, None),
            P(TOK, None),
        ),
        out_specs=(P(TOK, HEAD), P(TOK, HEAD)),
        check_vma=False,
    )
```

profile of v0, /device:TPU:6, one launch (start us, length us, event | category | flops | bytes accessed | tf_op | source)
XLA Modules:
  0.0 97.1 jit_solution(15237054021305085948)
XLA Ops:
  0.7 2.3 %kv.1.refs_7_ = bf16[128,256]{1,0:T(8,128)(2,1)} custom-call(bf16[128,1024]{1,0:T(8,128)(2,1)} %refs_0_.3, bf16[1024,128]{1,0:T(8,128)(2,1)} %refs_2_.5, bf16[1024,128]{1,0:T(8,128)(2,1)} %refs_3_.3), custom_call_target="tpu_custom_call" | custom-call | flops 10000000000 | bytes 1000000 | tf_op jit(solution)/shard_map/kv/pallas_call | solution.py:77
  5.6 7.9 %collective-permute-start.1 = (bf16[128,256]{1,0:T(8,128)(2,1)S(1)}, bf16[128,256]{1,0:T(8,128)(2,1)S(1)}, u32[]{:S(2)}, u32[]{:S(2)}) collective-permute-start(bf16[128,256]{1,0:T(8,128)(2,1)S(1)} %copy-done.9), channel_id=1, source_target_pairs={{0,15},{1,0},{2,1},{3,2},{4,3},{5,4},{6,5},{7,6},{8,7},{9,8},{10,9... | collective-permute-start | bytes 196616 | tf_op jit(solution)/shard_map/ppermute | solution.py:394
  13.5 1.6 %collective-permute-start.4 = (bf16[640,256]{1,0:T(8,128)(2,1)S(1)}, bf16[640,256]{1,0:T(8,128)(2,1)S(1)}, u32[]{:S(2)}, u32[]{:S(2)}) collective-permute-start(bf16[640,256]{1,0:T(8,128)(2,1)S(1)} %qd.1.refs_0_), channel_id=1, source_target_pairs={{0,16},{1,17},{2,18},{3,19},{4,20},{5,21},{6,22},{7,23},{8,24},{9,... | collective-permute-start | bytes 983048 | tf_op jit(solution)/shard_map/ppermute | solution.py:405
  16.4 3.4 %collective-permute-start.7 = (bf16[256,256]{1,0:T(8,128)(2,1)S(1)}, bf16[256,256]{1,0:T(8,128)(2,1)S(1)}, u32[]{:S(2)}, u32[]{:S(2)}) collective-permute-start(bf16[256,256]{1,0:T(8,128)(2,1)S(1)} %constant_dynamic-update-slice_fusion.refs_2_.refs_1_), channel_id=1, source_target_pairs={{0,6},{1,11},{2,8},{3,13},{4,10},{5,15},{6,12},{7,1},{8,14},{9,3},... | collective-permute-start | bytes 393224 | tf_op jit(solution)/shard_map/ppermute | solution.py:395
  19.8 2.1 %first_stats.2 = (f32[8,1280]{1,0:T(8,128)S(1)}, bf16[2560,256]{1,0:T(8,128)(2,1)S(1)}) custom-call(bf16[640,256]{1,0:T(8,128)(2,1)S(1)} %qd.1.refs_0_, bf16[640,256]{1,0:T(8,128)(2,1)S(1)} %collective-permute-done.3.refs_1_, bf16[256,256]{1,0:T(8,128)(2,1)S(1)} %constant_dynamic-update-slice_fusion.refs_2_.refs_1_), custom_call_target="tpu_custom_call" | custom-call | flops 10000000000 | bytes 1000000 | tf_op jit(solution)/shard_map/first_stats/pallas_call | solution.py:77
  22.6 2.0 %stats.2.refs_2_ = f32[8,1280]{1,0:T(8,128)S(1)} custom-call(bf16[256,256]{1,0:T(8,128)(2,1)S(1)} %collective-permute-done.2.refs_3_.refs_0_, bf16[2560,256]{1,0:T(8,128)(2,1)S(1)} %get-tuple-element.29.refs_1_.refs_2_, f32[8,1280]{1,0:T(8,128)S(1)} %get-tuple-element.31.refs_2_), custom_call_target="tpu_custom_call" | custom-call | flops 10000000000 | bytes 1000000 | tf_op jit(solution)/shard_map/stats/pallas_call | solution.py:77
  24.6 2.8 %collective-permute-done.6.refs_4_.refs_0_.refs_1_ = bf16[256,256]{1,0:T(8,128)(2,1)S(1)} collective-permute-done((bf16[256,256]{1,0:T(8,128)(2,1)S(1)}, bf16[256,256]{1,0:T(8,128)(2,1)S(1)}, u32[]{:S(2)}, u32[]{:S(2)}) %collective-permute-start.6) | collective-permute-done | bytes 131104 | tf_op jit(solution)/shard_map/ppermute | solution.py:395
  27.4 2.0 %stats.3.refs_3_ = f32[8,1280]{1,0:T(8,128)S(1)} custom-call(bf16[256,256]{1,0:T(8,128)(2,1)S(1)} %collective-permute-done.6.refs_4_.refs_0_.refs_1_, bf16[2560,256]{1,0:T(8,128)(2,1)S(1)} %get-tuple-element.29.refs_1_.refs_2_, f32[8,1280]{1,0:T(8,128)S(1)} %stats.2.refs_2_), custom_call_target="tpu_custom_call" | custom-call | flops 10000000000 | bytes 1000000 | tf_op jit(solution)/shard_map/stats/pallas_call | solution.py:77
  29.4 6.1 %first_stats.3 = (f32[8,1280]{1,0:T(8,128)S(1)}, bf16[2560,256]{1,0:T(8,128)(2,1)S(1)}) custom-call(bf16[640,256]{1,0:T(8,128)(2,1)S(1)} %collective-permute-done.4.refs_0_, bf16[640,256]{1,0:T(8,128)(2,1)S(1)} %collective-permute-done.5.refs_1_, bf16[256,256]{1,0:T(8,128)(2,1)S(1)} %constant_dynamic-update-slice_fusion.refs_2_.refs_1_, ...), custom_call_target="tpu_custom_call" | custom-call | flops 10000000000 | bytes 1000000 | tf_op jit(solution)/shard_map/first_stats/pallas_call | solution.py:77
  35.5 4.0 %both_stats.1.refs_0_.refs_4_ = f32[16,1280]{1,0:T(8,128)S(1)} custom-call(bf16[256,256]{1,0:T(8,128)(2,1)S(1)} %collective-permute-done.7.refs_0_, bf16[2560,256]{1,0:T(8,128)(2,1)S(1)} %get-tuple-element.29.refs_1_.refs_2_, bf16[2560,256]{1,0:T(8,128)(2,1)S(1)} %get-tuple-element.30.refs_2_.refs_3_, f32[8,1280]{1,0:T(8,128)S(1)} %stats.3.refs_3_, ...), custom_call_target="tpu_custom_call" | custom-call | flops 10000000000 | bytes 1000000 | tf_op jit(solution)/shard_map/both_stats/pallas_call | solution.py:77
  39.6 1.3 %collective-permute-done.8.refs_1_ = f32[16,1280]{1,0:T(8,128)S(1)} collective-permute-done((f32[16,1280]{1,0:T(8,128)S(1)}, f32[16,1280]{1,0:T(8,128)S(1)}, u32[]{:S(2)}, u32[]{:S(2)}) %collective-permute-start.8) | collective-permute-done | bytes 81952 | tf_op jit(solution)/shard_map/ppermute | solution.py:438
  40.9 1.7 %collective-permute-start.9 = (f32[16,1280]{1,0:T(8,128)S(1)}, f32[16,1280]{1,0:T(8,128)S(1)}, u32[]{:S(2)}, u32[]{:S(2)}) collective-permute-start(f32[16,1280]{1,0:T(8,128)S(1)} %merge.2.refs_0_), channel_id=1, source_target_pairs={{0,16},{1,17},{2,18},{3,19},{4,20},{5,21},{6,22},{7,23},{8,24},{9,... | collective-permute-start | bytes 245768 | tf_op jit(solution)/shard_map/ppermute | solution.py:438
  43.9 2.4 %collective-permute-start.11 = (bf16[256,384]{1,0:T(8,128)(2,1)S(1)}, bf16[256,384]{1,0:T(8,128)(2,1)S(1)}, u32[]{:S(2)}, u32[]{:S(2)}) collective-permute-start(bf16[256,384]{1,0:T(8,128)(2,1)S(1)} %get-tuple-element.38), channel_id=1, source_target_pairs={{0,128},{32,160},{64,192},{96,224},{128,0},{160,32},{192,64},{224,... | collective-permute-start | bytes 589832 | tf_op jit(solution)/shard_map/ppermute | solution.py:432
  46.3 4.1 %scores.2 = (bf16[512,5120]{1,0:T(8,128)(2,1)S(1)}, bf16[512,5120]{1,0:T(8,128)(2,1)S(1)}, f32[128,2560]{1,0:T(8,128)S(1)}) custom-call(bf16[256,256]{1,0:T(8,128)(2,1)S(1)} %collective-permute-done.7.refs_0_, bf16[256,256]{1,0:T(8,128)(2,1)S(1)} %collective-permute-done.6.refs_4_.refs_0_.refs_1_, bf16[2560,256]{1,0:T(8,128)(2,1)S(1)} %get-tuple-element.29.refs_1_.refs_2_, ...), custom_call_target="tpu_custom_call" | custom-call | flops 1500000000 | bytes 1000000 | tf_op jit(solution)/shard_map/scores/pallas_call | solution.py:77
  50.5 2.9 %pair.3 = (bf16[256,256]{1,0:T(8,128)(2,1)S(1)}, bf16[256,256]{1,0:T(8,128)(2,1)S(1)}) custom-call(bf16[512,5120]{1,0:T(8,128)(2,1)S(1)} %get-tuple-element.34.refs_0_, bf16[512,5120]{1,0:T(8,128)(2,1)S(1)} %get-tuple-element.35.refs_1_, bf16[2560,256]{1,0:T(8,128)(2,1)S(1)} %get-tuple-element.29.refs_1_.refs_2_, ...), custom_call_target="tpu_custom_call" | custom-call | flops 1500000000 | bytes 1000000 | tf_op jit(solution)/shard_map/pair/pallas_call | solution.py:77
  53.4 1.3 %collective-permute-start.16 = (bf16[256,256]{1,0:T(8,128)(2,1)S(1)}, bf16[256,256]{1,0:T(8,128)(2,1)S(1)}, u32[]{:S(2)}, u32[]{:S(2)}) collective-permute-start(bf16[256,256]{1,0:T(8,128)(2,1)S(1)} %get-tuple-element.36.refs_6_), channel_id=1, source_target_pairs={{6,0},{11,1},{8,2},{13,3},{10,4},{15,5},{12,6},{1,7},{14,8},{3,9},... | collective-permute-start | bytes 393224 | tf_op jit(solution)/shard_map/ppermute | solution.py:446
  54.7 1.3 %collective-permute-start.17 = (bf16[256,256]{1,0:T(8,128)(2,1)S(1)}, bf16[256,256]{1,0:T(8,128)(2,1)S(1)}, u32[]{:S(2)}, u32[]{:S(2)}) collective-permute-start(bf16[256,256]{1,0:T(8,128)(2,1)S(1)} %get-tuple-element.46), channel_id=1, source_target_pairs={{4,0},{13,1},{6,2},{15,3},{8,4},{1,5},{10,6},{3,7},{12,8},{5,9},{1... | collective-permute-start | bytes 393224 | tf_op jit(solution)/shard_map/ppermute | solution.py:446
  56.0 4.2 %scores.3 = (bf16[512,5120]{1,0:T(8,128)(2,1)S(1)}, bf16[512,5120]{1,0:T(8,128)(2,1)S(1)}, f32[128,640]{1,0:T(8,128)S(1)}, bf16[128,640]{1,0:T(8,128)(2,1)S(1)},...) custom-call(bf16[256,256]{1,0:T(8,128)(2,1)S(1)} %collective-permute-done.2.refs_3_.refs_0_, ...), custom_call_target="tpu_custom_call" | custom-call | flops 1500000000 | bytes 1000000 | tf_op jit(solution)/shard_map/scores/pallas_call | solution.py:77
  60.2 1.1 %collective-permute-start.13 = (bf16[128,640]{1,0:T(8,128)(2,1)S(1)}, bf16[128,640]{1,0:T(8,128)(2,1)S(1)}, u32[]{:S(2)}, u32[]{:S(2)}) collective-permute-start(bf16[128,640]{1,0:T(8,128)(2,1)S(1)} %get-tuple-element.41), channel_id=1, source_target_pairs={{0,16},{1,17},{2,18},{3,19},{4,20},{5,21},{6,22},{7,23},{8,24},{9,... | collective-permute-start | bytes 491528 | tf_op jit(solution)/shard_map/ppermute | solution.py:451
  62.4 2.2 %collective-permute-done.17.refs_5_.refs_2_ = bf16[256,256]{1,0:T(8,128)(2,1)S(1)} collective-permute-done((bf16[256,256]{1,0:T(8,128)(2,1)S(1)}, bf16[256,256]{1,0:T(8,128)(2,1)S(1)}, u32[]{:S(2)}, u32[]{:S(2)}) %collective-permute-start.17) | collective-permute-done | bytes 131104 | tf_op jit(solution)/shard_map/ppermute | solution.py:446
  64.6 1.5 %pair.4.refs_4_ = bf16[256,256]{1,0:T(8,128)(2,1)S(1)} custom-call(bf16[512,5120]{1,0:T(8,128)(2,1)S(1)} %get-tuple-element.44.refs_0_, bf16[512,5120]{1,0:T(8,128)(2,1)S(1)} %get-tuple-element.45.refs_1_, bf16[2560,256]{1,0:T(8,128)(2,1)S(1)} %get-tuple-element.29.refs_1_.refs_2_, bf16[2560,256]{1,0:T(8,128)(2,1)S(1)} %get-tuple-element.30.refs_2_.refs_3_, ...), custom_call_target="tpu_custom_call" | custom-call | flops 1500000000 | bytes 1000000 | tf_op jit(solution)/shard_map/pair/pallas_call | solution.py:77
  66.1 1.2 %collective-permute-start.21 = (bf16[256,256]{1,0:T(8,128)(2,1)S(1)}, bf16[256,256]{1,0:T(8,128)(2,1)S(1)}, u32[]{:S(2)}, u32[]{:S(2)}) collective-permute-start(bf16[256,256]{1,0:T(8,128)(2,1)S(1)} %pair.4.refs_4_), channel_id=1, source_target_pairs={{2,0},{15,1},{4,2},{1,3},{6,4},{3,5},{8,6},{5,7},{10,8},{7,9},{12,... | collective-permute-start | bytes 393224 | tf_op jit(solution)/shard_map/ppermute | solution.py:455
  67.3 1.5 %pair.5.refs_4_.refs_0_ = f32[256,256]{1,0:T(8,128)S(1)} custom-call(bf16[512,5120]{1,0:T(8,128)(2,1)S(1)} %get-tuple-element.44.refs_0_, bf16[512,5120]{1,0:T(8,128)(2,1)S(1)} %get-tuple-element.45.refs_1_, bf16[2560,256]{1,0:T(8,128)(2,1)S(1)} %get-tuple-element.29.refs_1_.refs_2_, bf16[2560,256]{1,0:T(8,128)(2,1)S(1)} %get-tuple-element.30.refs_2_.refs_3_, ...), custom_call_target="tpu_custom_call" | custom-call | flops 1500000000 | bytes 1000000 | tf_op jit(solution)/shard_map/pair/pallas_call | solution.py:77
  69.0 1.2 %collective-permute-start.20 = (bf16[128,640]{1,0:T(8,128)(2,1)S(1)}, bf16[128,640]{1,0:T(8,128)(2,1)S(1)}, u32[]{:S(2)}, u32[]{:S(2)}) collective-permute-start(bf16[128,640]{1,0:T(8,128)(2,1)S(1)} %get-tuple-element.47.refs_5_.refs_0_), channel_id=1, source_target_pairs={{0,192},{32,224},{64,0},{96,32},{128,64},{160,96},{192,128},{224,1... | collective-permute-start | bytes 491528 | tf_op jit(solution)/shard_map/ppermute | solution.py:478
  70.2 2.2 %collective-permute-start.18 = (bf16[128,640]{1,0:T(8,128)(2,1)S(1)}, bf16[128,640]{1,0:T(8,128)(2,1)S(1)}, u32[]{:S(2)}, u32[]{:S(2)}) collective-permute-start(bf16[128,640]{1,0:T(8,128)(2,1)S(1)} %get-tuple-element.47.refs_5_.refs_0_), channel_id=1, source_target_pairs={{0,64},{32,96},{64,128},{96,160},{128,192},{160,224},{192,0},{224,... | collective-permute-start | bytes 491528 | tf_op jit(solution)/shard_map/ppermute | solution.py:477
  72.4 1.9 %collective-permute-start.19 = (bf16[128,256]{1,0:T(8,128)(2,1)S(1)}, bf16[128,256]{1,0:T(8,128)(2,1)S(1)}, u32[]{:S(2)}, u32[]{:S(2)}) collective-permute-start(bf16[128,256]{1,0:T(8,128)(2,1)S(1)} %get-tuple-element.48), channel_id=1, source_target_pairs={{0,128},{32,160},{64,192},{96,224},{128,0},{160,32},{192,64},{224,... | collective-permute-start | bytes 196616 | tf_op jit(solution)/shard_map/ppermute | solution.py:479
  77.3 3.3 %collective-permute-done.23.refs_1_ = bf16[128,256]{1,0:T(8,128)(2,1)S(1)} collective-permute-done((bf16[128,256]{1,0:T(8,128)(2,1)S(1)}, bf16[128,256]{1,0:T(8,128)(2,1)S(1)}, u32[]{:S(2)}, u32[]{:S(2)}) %collective-permute-start.23) | collective-permute-done | bytes 65568 | tf_op jit(solution)/shard_map/ppermute | solution.py:460
  81.6 2.0 %collective-permute-start.25 = (bf16[128,256]{1,0:T(8,128)(2,1)S(1)}, bf16[128,256]{1,0:T(8,128)(2,1)S(1)}, u32[]{:S(2)}, u32[]{:S(2)}) collective-permute-start(bf16[128,256]{1,0:T(8,128)(2,1)S(1)} %piece_sum.1.refs_4_), channel_id=1, source_target_pairs={{0,128},{32,160},{64,192},{96,224},{128,0},{160,32},{192,64},{224,... | collective-permute-start | bytes 196616 | tf_op jit(solution)/shard_map/ppermute | solution.py:371
  85.0 2.4 %collective-permute-done.25.refs_6_ = bf16[128,256]{1,0:T(8,128)(2,1)S(1)} collective-permute-done((bf16[128,256]{1,0:T(8,128)(2,1)S(1)}, bf16[128,256]{1,0:T(8,128)(2,1)S(1)}, u32[]{:S(2)}, u32[]{:S(2)}) %collective-permute-start.25) | collective-permute-done | bytes 65568 | tf_op jit(solution)/shard_map/ppermute | solution.py:371
  87.4 1.7 %collective-permute-done.26.refs_7_ = bf16[128,256]{1,0:T(8,128)(2,1)S(1)} collective-permute-done((bf16[128,256]{1,0:T(8,128)(2,1)S(1)}, bf16[128,256]{1,0:T(8,128)(2,1)S(1)}, u32[]{:S(2)}, u32[]{:S(2)}) %collective-permute-start.26) | collective-permute-done | bytes 65568 | tf_op jit(solution)/shard_map/ppermute | solution.py:371
  89.5 3.1 %collective-permute-start.28 = (bf16[640,128]{1,0:T(8,128)(2,1)S(1)}, bf16[640,128]{1,0:T(8,128)(2,1)S(1)}, u32[]{:S(2)}, u32[]{:S(2)}) collective-permute-start(bf16[640,128]{1,0:T(8,128)(2,1)S(1)} %get-tuple-element.55), channel_id=1, source_target_pairs={{0,32},{32,0},{64,96},{96,64},{128,160},{160,128},{192,224},{224,1... | collective-permute-start | bytes 491528 | tf_op jit(solution)/shard_map/ppermute | solution.py:501
  92.6 3.8 %collective-permute-done.28.refs_1_ = bf16[640,128]{1,0:T(8,128)(2,1)S(1)} collective-permute-done((bf16[640,128]{1,0:T(8,128)(2,1)S(1)}, bf16[640,128]{1,0:T(8,128)(2,1)S(1)}, u32[]{:S(2)}, u32[]{:S(2)}) %collective-permute-start.28) | collective-permute-done | bytes 163872 | tf_op jit(solution)/shard_map/ppermute | solution.py:501
  (72 shorter events, 13.6 us)
Async XLA Ops:
  0.7 2.4 %copy-start.4 = (bf16[128,1024]{1,0:T(8,128)(2,1)S(1)}, bf16[128,1024]{1,0:T(8,128)(2,1)}, u32[]{:S(2)}) copy-start(bf16[128,1024]{1,0:T(8,128)(2,1)} %refs_5_.1) | copy-start | bytes 786436
  4.8 15.0 %collective-permute-start.3 = (bf16[640,256]{1,0:T(8,128)(2,1)S(1)}, bf16[640,256]{1,0:T(8,128)(2,1)S(1)}, u32[]{:S(2)}, u32[]{:S(2)}) collective-permute-start(bf16[640,256]{1,0:T(8,128)(2,1)S(1)} %qd.1.refs_0_), channel_id=1, source_target_pairs={{0,1},{1,0},{2,3},{3,2},{4,5},{5,4},{6,7},{7,6},{8,9},{9,8},{10,11... | collective-permute-start | bytes 983048 | tf_op jit(solution)/shard_map/ppermute | solution.py:404
  4.9 10.2 %collective-permute-start = (bf16[128,256]{1,0:T(8,128)(2,1)S(1)}, bf16[128,256]{1,0:T(8,128)(2,1)S(1)}, u32[]{:S(2)}, u32[]{:S(2)}) collective-permute-start(bf16[128,256]{1,0:T(8,128)(2,1)S(1)} %copy-done.9), channel_id=1, source_target_pairs={{0,0},{1,15},{2,2},{3,1},{4,4},{5,3},{6,6},{7,5},{8,8},{9,7},{10,1... | collective-permute-start | bytes 196616 | tf_op jit(solution)/shard_map/ppermute | solution.py:394
  5.6 9.8 %collective-permute-start.1 = (bf16[128,256]{1,0:T(8,128)(2,1)S(1)}, bf16[128,256]{1,0:T(8,128)(2,1)S(1)}, u32[]{:S(2)}, u32[]{:S(2)}) collective-permute-start(bf16[128,256]{1,0:T(8,128)(2,1)S(1)} %copy-done.9), channel_id=1, source_target_pairs={{0,15},{1,0},{2,1},{3,2},{4,3},{5,4},{6,5},{7,6},{8,7},{9,8},{10,9... | collective-permute-start | bytes 196616 | tf_op jit(solution)/shard_map/ppermute | solution.py:394
  13.5 9.1 %collective-permute-start.4 = (bf16[640,256]{1,0:T(8,128)(2,1)S(1)}, bf16[640,256]{1,0:T(8,128)(2,1)S(1)}, u32[]{:S(2)}, u32[]{:S(2)}) collective-permute-start(bf16[640,256]{1,0:T(8,128)(2,1)S(1)} %qd.1.refs_0_), channel_id=1, source_target_pairs={{0,16},{1,17},{2,18},{3,19},{4,20},{5,21},{6,22},{7,23},{8,24},{9,... | collective-permute-start | bytes 983048 | tf_op jit(solution)/shard_map/ppermute | solution.py:405
  15.4 7.2 %collective-permute-start.2 = (bf16[256,256]{1,0:T(8,128)(2,1)S(1)}, bf16[256,256]{1,0:T(8,128)(2,1)S(1)}, u32[]{:S(2)}, u32[]{:S(2)}) collective-permute-start(bf16[256,256]{1,0:T(8,128)(2,1)S(1)} %constant_dynamic-update-slice_fusion.refs_2_.refs_1_), channel_id=1, source_target_pairs={{0,2},{1,15},{2,4},{3,1},{4,6},{5,3},{6,8},{7,5},{8,10},{9,7},{10,... | collective-permute-start | bytes 393224 | tf_op jit(solution)/shard_map/ppermute | solution.py:395
  16.4 11.0 %collective-permute-start.6 = (bf16[256,256]{1,0:T(8,128)(2,1)S(1)}, bf16[256,256]{1,0:T(8,128)(2,1)S(1)}, u32[]{:S(2)}, u32[]{:S(2)}) collective-permute-start(bf16[256,256]{1,0:T(8,128)(2,1)S(1)} %constant_dynamic-update-slice_fusion.refs_2_.refs_1_), channel_id=1, source_target_pairs={{0,4},{1,13},{2,6},{3,15},{4,8},{5,1},{6,10},{7,3},{8,12},{9,5},{1... | collective-permute-start | bytes 393224 | tf_op jit(solution)/shard_map/ppermute | solution.py:395
  16.4 19.1 %collective-permute-start.7 = (bf16[256,256]{1,0:T(8,128)(2,1)S(1)}, bf16[256,256]{1,0:T(8,128)(2,1)S(1)}, u32[]{:S(2)}, u32[]{:S(2)}) collective-permute-start(bf16[256,256]{1,0:T(8,128)(2,1)S(1)} %constant_dynamic-update-slice_fusion.refs_2_.refs_1_), channel_id=1, source_target_pairs={{0,6},{1,11},{2,8},{3,13},{4,10},{5,15},{6,12},{7,1},{8,14},{9,3},... | collective-permute-start | bytes 393224 | tf_op jit(solution)/shard_map/ppermute | solution.py:395
  22.6 6.8 %collective-permute-start.5 = (bf16[640,256]{1,0:T(8,128)(2,1)S(1)}, bf16[640,256]{1,0:T(8,128)(2,1)S(1)}, u32[]{:S(2)}, u32[]{:S(2)}) collective-permute-start(bf16[640,256]{1,0:T(8,128)(2,1)S(1)} %collective-permute-done.4.refs_0_), channel_id=1, source_target_pairs={{0,1},{1,0},{2,3},{3,2},{4,5},{5,4},{6,7},{7,6},{8,9},{9,8},{10,11... | collective-permute-start | bytes 983048 | tf_op jit(solution)/shard_map/ppermute | solution.py:406
  39.5 3.1 %copy-start.5 = (bf16[1024,128]{1,0:T(8,128)(2,1)S(1)}, bf16[1024,128]{1,0:T(8,128)(2,1)}, u32[]{:S(2)}) copy-start(bf16[1024,128]{1,0:T(8,128)(2,1)} %refs_2_.5) | copy-start | bytes 786436
  39.5 3.1 %copy-start.6 = (bf16[1024,128]{1,0:T(8,128)(2,1)S(1)}, bf16[1024,128]{1,0:T(8,128)(2,1)}, u32[]{:S(2)}) copy-start(bf16[1024,128]{1,0:T(8,128)(2,1)} %refs_3_.3) | copy-start | bytes 786436
  39.5 1.4 %collective-permute-start.8 = (f32[16,1280]{1,0:T(8,128)S(1)}, f32[16,1280]{1,0:T(8,128)S(1)}, u32[]{:S(2)}, u32[]{:S(2)}) collective-permute-start(f32[16,1280]{1,0:T(8,128)S(1)} %both_stats.1.refs_0_.refs_4_), channel_id=1, source_target_pairs={{0,1},{1,0},{2,3},{3,2},{4,5},{5,4},{6,7},{7,6},{8,9},{9,8},{10,11... | collective-permute-start | bytes 245768 | tf_op jit(solution)/shard_map/ppermute | solution.py:438
  40.9 5.4 %collective-permute-start.9 = (f32[16,1280]{1,0:T(8,128)S(1)}, f32[16,1280]{1,0:T(8,128)S(1)}, u32[]{:S(2)}, u32[]{:S(2)}) collective-permute-start(f32[16,1280]{1,0:T(8,128)S(1)} %merge.2.refs_0_), channel_id=1, source_target_pairs={{0,16},{1,17},{2,18},{3,19},{4,20},{5,21},{6,22},{7,23},{8,24},{9,... | collective-permute-start | bytes 245768 | tf_op jit(solution)/shard_map/ppermute | solution.py:438
  43.3 12.7 %collective-permute-start.10 = (bf16[256,384]{1,0:T(8,128)(2,1)S(1)}, bf16[256,384]{1,0:T(8,128)(2,1)S(1)}, u32[]{:S(2)}, u32[]{:S(2)}) collective-permute-start(bf16[256,384]{1,0:T(8,128)(2,1)S(1)} %get-tuple-element.37), channel_id=1, source_target_pairs={{0,64},{32,96},{64,128},{96,160},{128,192},{160,224},{192,0},{224,... | collective-permute-start | bytes 589832 | tf_op jit(solution)/shard_map/ppermute | solution.py:432
  43.9 12.2 %collective-permute-start.11 = (bf16[256,384]{1,0:T(8,128)(2,1)S(1)}, bf16[256,384]{1,0:T(8,128)(2,1)S(1)}, u32[]{:S(2)}, u32[]{:S(2)}) collective-permute-start(bf16[256,384]{1,0:T(8,128)(2,1)S(1)} %get-tuple-element.38), channel_id=1, source_target_pairs={{0,128},{32,160},{64,192},{96,224},{128,0},{160,32},{192,64},{224,... | collective-permute-start | bytes 589832 | tf_op jit(solution)/shard_map/ppermute | solution.py:432
  46.3 9.7 %collective-permute-start.12 = (bf16[256,384]{1,0:T(8,128)(2,1)S(1)}, bf16[256,384]{1,0:T(8,128)(2,1)S(1)}, u32[]{:S(2)}, u32[]{:S(2)}) collective-permute-start(bf16[256,384]{1,0:T(8,128)(2,1)S(1)} %get-tuple-element.39), channel_id=1, source_target_pairs={{0,192},{32,224},{64,0},{96,32},{128,64},{160,96},{192,128},{224,1... | collective-permute-start | bytes 589832 | tf_op jit(solution)/shard_map/ppermute | solution.py:432
  53.4 9.1 %collective-permute-start.16 = (bf16[256,256]{1,0:T(8,128)(2,1)S(1)}, bf16[256,256]{1,0:T(8,128)(2,1)S(1)}, u32[]{:S(2)}, u32[]{:S(2)}) collective-permute-start(bf16[256,256]{1,0:T(8,128)(2,1)S(1)} %get-tuple-element.36.refs_6_), channel_id=1, source_target_pairs={{6,0},{11,1},{8,2},{13,3},{10,4},{15,5},{12,6},{1,7},{14,8},{3,9},... | collective-permute-start | bytes 393224 | tf_op jit(solution)/shard_map/ppermute | solution.py:446
  54.7 9.9 %collective-permute-start.17 = (bf16[256,256]{1,0:T(8,128)(2,1)S(1)}, bf16[256,256]{1,0:T(8,128)(2,1)S(1)}, u32[]{:S(2)}, u32[]{:S(2)}) collective-permute-start(bf16[256,256]{1,0:T(8,128)(2,1)S(1)} %get-tuple-element.46), channel_id=1, source_target_pairs={{4,0},{13,1},{6,2},{15,3},{8,4},{1,5},{10,6},{3,7},{12,8},{5,9},{1... | collective-permute-start | bytes 393224 | tf_op jit(solution)/shard_map/ppermute | solution.py:446
  60.2 8.7 %collective-permute-start.13 = (bf16[128,640]{1,0:T(8,128)(2,1)S(1)}, bf16[128,640]{1,0:T(8,128)(2,1)S(1)}, u32[]{:S(2)}, u32[]{:S(2)}) collective-permute-start(bf16[128,640]{1,0:T(8,128)(2,1)S(1)} %get-tuple-element.41), channel_id=1, source_target_pairs={{0,16},{1,17},{2,18},{3,19},{4,20},{5,21},{6,22},{7,23},{8,24},{9,... | collective-permute-start | bytes 491528 | tf_op jit(solution)/shard_map/ppermute | solution.py:451
  61.3 7.6 %collective-permute-start.14 = (bf16[128,640]{1,0:T(8,128)(2,1)S(1)}, bf16[128,640]{1,0:T(8,128)(2,1)S(1)}, u32[]{:S(2)}, u32[]{:S(2)}) collective-permute-start(bf16[128,640]{1,0:T(8,128)(2,1)S(1)} %get-tuple-element.42), channel_id=1, source_target_pairs={{0,17},{1,16},{2,19},{3,18},{4,21},{5,20},{6,23},{7,22},{8,25},{9,... | collective-permute-start | bytes 491528 | tf_op jit(solution)/shard_map/ppermute | solution.py:451
  61.3 7.6 %collective-permute-start.15 = (bf16[128,640]{1,0:T(8,128)(2,1)S(1)}, bf16[128,640]{1,0:T(8,128)(2,1)S(1)}, u32[]{:S(2)}, u32[]{:S(2)}) collective-permute-start(bf16[128,640]{1,0:T(8,128)(2,1)S(1)} %get-tuple-element.43), channel_id=1, source_target_pairs={{0,1},{1,0},{2,3},{3,2},{4,5},{5,4},{6,7},{7,6},{8,9},{9,8},{10,11... | collective-permute-start | bytes 491528 | tf_op jit(solution)/shard_map/ppermute | solution.py:451
  66.1 8.2 %collective-permute-start.21 = (bf16[256,256]{1,0:T(8,128)(2,1)S(1)}, bf16[256,256]{1,0:T(8,128)(2,1)S(1)}, u32[]{:S(2)}, u32[]{:S(2)}) collective-permute-start(bf16[256,256]{1,0:T(8,128)(2,1)S(1)} %pair.4.refs_4_), channel_id=1, source_target_pairs={{2,0},{15,1},{4,2},{1,3},{6,4},{3,5},{8,6},{5,7},{10,8},{7,9},{12,... | collective-permute-start | bytes 393224 | tf_op jit(solution)/shard_map/ppermute | solution.py:455
  69.0 8.0 %collective-permute-start.20 = (bf16[128,640]{1,0:T(8,128)(2,1)S(1)}, bf16[128,640]{1,0:T(8,128)(2,1)S(1)}, u32[]{:S(2)}, u32[]{:S(2)}) collective-permute-start(bf16[128,640]{1,0:T(8,128)(2,1)S(1)} %get-tuple-element.47.refs_5_.refs_0_), channel_id=1, source_target_pairs={{0,192},{32,224},{64,0},{96,32},{128,64},{160,96},{192,128},{224,1... | collective-permute-start | bytes 491528 | tf_op jit(solution)/shard_map/ppermute | solution.py:478
  70.2 14.0 %collective-permute-start.18 = (bf16[128,640]{1,0:T(8,128)(2,1)S(1)}, bf16[128,640]{1,0:T(8,128)(2,1)S(1)}, u32[]{:S(2)}, u32[]{:S(2)}) collective-permute-start(bf16[128,640]{1,0:T(8,128)(2,1)S(1)} %get-tuple-element.47.refs_5_.refs_0_), channel_id=1, source_target_pairs={{0,64},{32,96},{64,128},{96,160},{128,192},{160,224},{192,0},{224,... | collective-permute-start | bytes 491528 | tf_op jit(solution)/shard_map/ppermute | solution.py:477
  72.4 11.2 %collective-permute-start.19 = (bf16[128,256]{1,0:T(8,128)(2,1)S(1)}, bf16[128,256]{1,0:T(8,128)(2,1)S(1)}, u32[]{:S(2)}, u32[]{:S(2)}) collective-permute-start(bf16[128,256]{1,0:T(8,128)(2,1)S(1)} %get-tuple-element.48), channel_id=1, source_target_pairs={{0,128},{32,160},{64,192},{96,224},{128,0},{160,32},{192,64},{224,... | collective-permute-start | bytes 196616 | tf_op jit(solution)/shard_map/ppermute | solution.py:479
  74.4 2.9 %collective-permute-start.22 = (bf16[128,256]{1,0:T(8,128)(2,1)S(1)}, bf16[128,256]{1,0:T(8,128)(2,1)S(1)}, u32[]{:S(2)}, u32[]{:S(2)}) collective-permute-start(bf16[128,256]{1,0:T(8,128)(2,1)S(1)} %get-tuple-element.49), channel_id=1, source_target_pairs={{0,0},{15,1},{2,2},{1,3},{4,4},{3,5},{6,6},{5,7},{8,8},{7,9},{10,1... | collective-permute-start | bytes 196616 | tf_op jit(solution)/shard_map/ppermute | solution.py:460
  75.1 5.5 %collective-permute-start.23 = (bf16[128,256]{1,0:T(8,128)(2,1)S(1)}, bf16[128,256]{1,0:T(8,128)(2,1)S(1)}, u32[]{:S(2)}, u32[]{:S(2)}) collective-permute-start(bf16[128,256]{1,0:T(8,128)(2,1)S(1)} %get-tuple-element.50), channel_id=1, source_target_pairs={{15,0},{0,1},{1,2},{2,3},{3,4},{4,5},{5,6},{6,7},{7,8},{8,9},{9,10... | collective-permute-start | bytes 196616 | tf_op jit(solution)/shard_map/ppermute | solution.py:460
  77.0 7.1 %collective-permute-start.27 = (bf16[128,384]{1,0:T(8,128)(2,1)S(1)}, bf16[128,384]{1,0:T(8,128)(2,1)S(1)}, u32[]{:S(2)}, u32[]{:S(2)}) collective-permute-start(bf16[128,384]{1,0:T(8,128)(2,1)S(1)} %slice.4), channel_id=1, source_target_pairs={{0,192},{32,224},{64,0},{96,32},{128,64},{160,96},{192,128},{224,1... | collective-permute-start | bytes 294920 | tf_op jit(solution)/shard_map/ppermute | solution.py:480
  80.6 4.3 %collective-permute-start.24 = (bf16[128,256]{1,0:T(8,128)(2,1)S(1)}, bf16[128,256]{1,0:T(8,128)(2,1)S(1)}, u32[]{:S(2)}, u32[]{:S(2)}) collective-permute-start(bf16[128,256]{1,0:T(8,128)(2,1)S(1)} %piece_sum.1.refs_4_), channel_id=1, source_target_pairs={{0,64},{32,96},{64,128},{96,160},{128,192},{160,224},{192,0},{224,... | collective-permute-start | bytes 196616 | tf_op jit(solution)/shard_map/ppermute | solution.py:371
  81.6 5.8 %collective-permute-start.25 = (bf16[128,256]{1,0:T(8,128)(2,1)S(1)}, bf16[128,256]{1,0:T(8,128)(2,1)S(1)}, u32[]{:S(2)}, u32[]{:S(2)}) collective-permute-start(bf16[128,256]{1,0:T(8,128)(2,1)S(1)} %piece_sum.1.refs_4_), channel_id=1, source_target_pairs={{0,128},{32,160},{64,192},{96,224},{128,0},{160,32},{192,64},{224,... | collective-permute-start | bytes 196616 | tf_op jit(solution)/shard_map/ppermute | solution.py:371
  83.6 5.5 %collective-permute-start.26 = (bf16[128,256]{1,0:T(8,128)(2,1)S(1)}, bf16[128,256]{1,0:T(8,128)(2,1)S(1)}, u32[]{:S(2)}, u32[]{:S(2)}) collective-permute-start(bf16[128,256]{1,0:T(8,128)(2,1)S(1)} %piece_sum.1.refs_4_), channel_id=1, source_target_pairs={{0,192},{32,224},{64,0},{96,32},{128,64},{160,96},{192,128},{224,1... | collective-permute-start | bytes 196616 | tf_op jit(solution)/shard_map/ppermute | solution.py:371
  89.5 6.9 %collective-permute-start.28 = (bf16[640,128]{1,0:T(8,128)(2,1)S(1)}, bf16[640,128]{1,0:T(8,128)(2,1)S(1)}, u32[]{:S(2)}, u32[]{:S(2)}) collective-permute-start(bf16[640,128]{1,0:T(8,128)(2,1)S(1)} %get-tuple-element.55), channel_id=1, source_target_pairs={{0,32},{32,0},{64,96},{96,64},{128,160},{160,128},{192,224},{224,1... | collective-permute-start | bytes 491528 | tf_op jit(solution)/shard_map/ppermute | solution.py:501
  (7 other events, 13.5 us)
where the time goes:
time: 97.3 us; the launch traced here: 97.1 us
  starting transfers between devices  39 us (40%)
  Pallas kernels  36.5 us (38%)
  waiting for transfers between devices  19.6 us (20%)
    pallas_call x22, Pallas kernels, call(): pl.pallas_call(kernel, out_shape=tuple(outs), in_specs=[spec(i) for i in...  36.5 us
    ppermute x2, starting transfers between devices, per_device(): lax.ppermute(kv, TOK, perm)  8.58 us
    ppermute x3, waiting for transfers between devices, over_x(): lax.ppermute(array, HEAD, SHIFT_X[r])  4.55 us
    ppermute x3, starting transfers between devices, per_device(): lax.ppermute(block, TOK, FORTH[j])  4.38 us
    ppermute x1, waiting for transfers between devices, per_device(): lax.ppermute(theirs, HEAD, SWAP_YH)  3.79 us
    ppermute x3, starting transfers between devices, over_x(): lax.ppermute(array, HEAD, SHIFT_X[r])  3.53 us
    ppermute x2, waiting for transfers between devices, per_device(): lax.ppermute(piece, TOK, perm)  3.33 us
    ppermute x1, starting transfers between devices, per_device(): lax.ppermute(theirs, HEAD, SWAP_YH)  3.11 us
  transfers between devices with their start and end apart: 29, of which 11 were waited for; matrix products, arithmetic and copies ran while one was open for 0% of the time, Pallas kernels for 29%

commit v1 on v0

--- a/solution.py
+++ b/solution.py
@@ -122,20 +122,17 @@
     total = rhs.shape[0] // 2
     keys = kv[:, 0:128]
     values = kv[:, 128:256]
-
-    @pl.loop(0, total // 256)
-    def _(index):
-        tile = pl.multiple_of(index * 256, 256)
-        cols = pl.ds(tile, 256)
+    for tile in range(0, total, 256):
+        cols = slice(tile, tile + 256)
         for h in range(2):
-            rows = pl.ds(pl.multiple_of(h * total + tile, 256), 256)
-            s = dot(keys, rhs[rows, 0:128], 1, 1)
+            lo = h * total + tile
+            s = dot(keys, rhs[lo : lo + 256, 0:128], 1, 1)
             peak = jnp.max(s, axis=0, keepdims=True) * LOG2E
             if before is not None:
                 old_peak = before[h : h + 1, cols]
                 peak = jnp.maximum(peak, old_peak)
             e = jnp.exp2(s * LOG2E - peak)
-            dp = dot(values, rhs[rows, 128:256], 1, 1)
+            dp = dot(values, rhs[lo : lo + 256, 128:256], 1, 1)
             norm = jnp.sum(e, axis=0, keepdims=True)
             mass = jnp.sum(e * dp, axis=0, keepdims=True)
             if before is not None:
@@ -146,13 +143,11 @@
             out[2 + h : 3 + h, cols] = norm
             out[4 + h : 5 + h, cols] = mass
 
-    out[6:8, :] = jnp.zeros((2, total), F32)
-
 
 def first_stats_kernel(count, *refs):
     first, second = refs[:2]
     blocks = refs[2 : 2 + count]
-    stats, rhs = refs[2 + count :]
+    stats, rhs, kv = refs[2 + count :]
     half = first.shape[0]
     lane = lax.broadcasted_iota(jnp.int32, (1, 256), 1)
     for h in range(2):
@@ -161,8 +156,17 @@
             x = rows[...]
             lo = (2 * h + part) * half
             rhs[lo : lo + half, :] = jnp.where(keep, x, jnp.zeros_like(x))
-    for i, kv in enumerate(blocks):
-        stats_block(kv, rhs, stats if i else None, stats)
+    stats[0:2, :] = jnp.full((2, 2 * half), -1e30, F32)
+    stats[2:8, :] = jnp.zeros((6, 2 * half), F32)
+    if count == 1:
+        stats_block(blocks[0], rhs, None, stats)
+        return
+    for i, block in enumerate(blocks):
+        kv[i] = block[...]
+
+    @pl.loop(0, count)
+    def _(i):
+        stats_block(kv.at[i], rhs, stats, stats)
 
 
 def first_stats(first, second, blocks):
@@ -172,14 +176,18 @@
         [sds((8, total), F32), sds((2 * total, 256), BF16)],
         [first, second, *blocks],
         "first_stats",
+        scratch=[pltpu.VMEM((len(blocks), *blocks[0].shape), BF16)],
     )
 
 
 def next_stats_kernel(kv, rhs, before, stats):
+    stats[6:8, :] = jnp.zeros((2, stats.shape[1]), F32)
     stats_block(kv, rhs, before, stats)
 
 
 def both_stats_kernel(kv, rhs_a, rhs_b, before_a, before_b, stats):
+    for lo in (6, 14):
+        stats[lo : lo + 2, :] = jnp.zeros((2, stats.shape[1]), F32)
     stats_block(kv, rhs_a, before_a, stats.at[0:8])
     stats_block(kv, rhs_b, before_b, stats.at[8:16])
 

time: 97.3 us -> 91.4 us (0.939)
  Pallas kernels: 36.5 us -> 29.1 us
    pallas_call x22, Pallas kernels: 36.5 us -> 29.1 us  [call(): pl.pallas_call(kernel, out_shape=tuple(outs), in_specs=[spec(i) for i in...]
    ppermute x1, waiting for transfers between devices: 2.18 us -> 0.01 us  [per_device(): lax.ppermute(dkv_2, TOK, BACK[2])]
    ppermute x1, waiting for transfers between devices: 0.01 us -> 1.84 us  [per_device(): lax.ppermute(dkv_3, TOK, BACK[3])]
    ppermute x3, waiting for transfers between devices: 0.01 us -> 1.76 us  [per_device(): lax.ppermute(x_weights[r], HEAD, SHIFT_X[r])]
    ppermute x1, starting transfers between devices: 1.35 us -> 0.08 us  [per_device(): lax.ppermute(dkv_3, TOK, BACK[3])]
    ppermute x3, starting transfers between devices: 3.53 us -> 4.75 us  [over_x(): lax.ppermute(array, HEAD, SHIFT_X[r])]
  transfers between devices with their start and end apart: 29 -> 29, of which waited for: 11 -> 11; matrix products, arithmetic and copies ran while one was open for 0% -> 0% of each run, Pallas kernels for 29% -> 25%
where the time goes in v1:
time: 91.4 us; the launch traced here: 91.2 us
  starting transfers between devices  39.7 us (43%)
  Pallas kernels  29.1 us (32%)
  waiting for transfers between devices  20.5 us (22%)
  between operations  0.97 us (1%)
    pallas_call x22, Pallas kernels, call(): pl.pallas_call(kernel, out_shape=tuple(outs), in_specs=[spec(i) for i in...  29.1 us
    ppermute x2, starting transfers between devices, per_device(): lax.ppermute(kv, TOK, perm)  8.58 us
    ppermute x3, starting transfers between devices, over_x(): lax.ppermute(array, HEAD, SHIFT_X[r])  4.75 us
    ppermute x3, starting transfers between devices, per_device(): lax.ppermute(block, TOK, FORTH[j])  4.38 us
    ppermute x3, waiting for transfers between devices, over_x(): lax.ppermute(array, HEAD, SHIFT_X[r])  3.78 us
    ppermute x3, waiting for transfers between devices, per_device(): lax.ppermute(block, TOK, FORTH[j])  3.72 us
    ppermute x1, waiting for transfers between devices, per_device(): lax.ppermute(theirs, HEAD, SWAP_YH)  3.67 us
    ppermute x1, starting transfers between devices, per_device(): lax.ppermute(theirs, HEAD, SWAP_YH)  3.23 us
  transfers between devices with their start and end apart: 29, of which 11 were waited for; matrix products, arithmetic and copies ran while one was open for 0% of the time, Pallas kernels for 25%

profile of v1, /device:TPU:6, one launch (start us, length us, event | category | flops | bytes accessed | tf_op | source)
XLA Modules:
  0.0 91.2 jit_solution(12195782852913014645)
XLA Ops:
  0.7 2.3 %kv.1.refs_7_ = bf16[128,256]{1,0:T(8,128)(2,1)} custom-call(bf16[128,1024]{1,0:T(8,128)(2,1)} %refs_0_.3, bf16[1024,128]{1,0:T(8,128)(2,1)} %refs_2_.5, bf16[1024,128]{1,0:T(8,128)(2,1)} %refs_3_.3), custom_call_target="tpu_custom_call" | custom-call | flops 10000000000 | bytes 1000000 | tf_op jit(solution)/shard_map/kv/pallas_call | solution.py:77
  5.6 7.9 %collective-permute-start.1 = (bf16[128,256]{1,0:T(8,128)(2,1)S(1)}, bf16[128,256]{1,0:T(8,128)(2,1)S(1)}, u32[]{:S(2)}, u32[]{:S(2)}) collective-permute-start(bf16[128,256]{1,0:T(8,128)(2,1)S(1)} %copy-done.9), channel_id=1, source_target_pairs={{0,15},{1,0},{2,1},{3,2},{4,3},{5,4},{6,5},{7,6},{8,7},{9,8},{10,9... | collective-permute-start | bytes 196616 | tf_op jit(solution)/shard_map/ppermute | solution.py:402
  13.5 1.6 %collective-permute-start.4 = (bf16[640,256]{1,0:T(8,128)(2,1)S(1)}, bf16[640,256]{1,0:T(8,128)(2,1)S(1)}, u32[]{:S(2)}, u32[]{:S(2)}) collective-permute-start(bf16[640,256]{1,0:T(8,128)(2,1)S(1)} %qd.1.refs_0_), channel_id=1, source_target_pairs={{0,16},{1,17},{2,18},{3,19},{4,20},{5,21},{6,22},{7,23},{8,24},{9,... | collective-permute-start | bytes 983048 | tf_op jit(solution)/shard_map/ppermute | solution.py:413
  16.4 3.4 %collective-permute-start.7 = (bf16[256,256]{1,0:T(8,128)(2,1)S(1)}, bf16[256,256]{1,0:T(8,128)(2,1)S(1)}, u32[]{:S(2)}, u32[]{:S(2)}) collective-permute-start(bf16[256,256]{1,0:T(8,128)(2,1)S(1)} %constant_dynamic-update-slice_fusion.refs_2_.refs_1_), channel_id=1, source_target_pairs={{0,6},{1,11},{2,8},{3,13},{4,10},{5,15},{6,12},{7,1},{8,14},{9,3},... | collective-permute-start | bytes 393224 | tf_op jit(solution)/shard_map/ppermute | solution.py:403
  19.8 1.2 %first_stats.2 = (f32[8,1280]{1,0:T(8,128)S(1)}, bf16[2560,256]{1,0:T(8,128)(2,1)S(1)}) custom-call(bf16[640,256]{1,0:T(8,128)(2,1)S(1)} %qd.1.refs_0_, bf16[640,256]{1,0:T(8,128)(2,1)S(1)} %collective-permute-done.3.refs_1_, bf16[256,256]{1,0:T(8,128)(2,1)S(1)} %constant_dynamic-update-slice_fusion.refs_2_.refs_1_), custom_call_target="tpu_custom_call" | custom-call | flops 10000000000 | bytes 1000000 | tf_op jit(solution)/shard_map/first_stats/pallas_call | solution.py:77
  21.0 1.6 %collective-permute-done.4.refs_0_ = bf16[640,256]{1,0:T(8,128)(2,1)S(1)} collective-permute-done((bf16[640,256]{1,0:T(8,128)(2,1)S(1)}, bf16[640,256]{1,0:T(8,128)(2,1)S(1)}, u32[]{:S(2)}, u32[]{:S(2)}) %collective-permute-start.4) | collective-permute-done | bytes 327712 | tf_op jit(solution)/shard_map/ppermute | solution.py:413
  23.7 3.7 %collective-permute-done.6.refs_4_.refs_0_.refs_1_ = bf16[256,256]{1,0:T(8,128)(2,1)S(1)} collective-permute-done((bf16[256,256]{1,0:T(8,128)(2,1)S(1)}, bf16[256,256]{1,0:T(8,128)(2,1)S(1)}, u32[]{:S(2)}, u32[]{:S(2)}) %collective-permute-start.6) | collective-permute-done | bytes 131104 | tf_op jit(solution)/shard_map/ppermute | solution.py:403
  27.4 1.1 %stats.3.refs_3_ = f32[8,1280]{1,0:T(8,128)S(1)} custom-call(bf16[256,256]{1,0:T(8,128)(2,1)S(1)} %collective-permute-done.6.refs_4_.refs_0_.refs_1_, bf16[2560,256]{1,0:T(8,128)(2,1)S(1)} %get-tuple-element.29.refs_1_.refs_2_, f32[8,1280]{1,0:T(8,128)S(1)} %stats.2.refs_2_), custom_call_target="tpu_custom_call" | custom-call | flops 10000000000 | bytes 1000000 | tf_op jit(solution)/shard_map/stats/pallas_call | solution.py:77
  28.5 3.3 %first_stats.3 = (f32[8,1280]{1,0:T(8,128)S(1)}, bf16[2560,256]{1,0:T(8,128)(2,1)S(1)}) custom-call(bf16[640,256]{1,0:T(8,128)(2,1)S(1)} %collective-permute-done.4.refs_0_, bf16[640,256]{1,0:T(8,128)(2,1)S(1)} %collective-permute-done.5.refs_1_, bf16[256,256]{1,0:T(8,128)(2,1)S(1)} %constant_dynamic-update-slice_fusion.refs_2_.refs_1_, ...), custom_call_target="tpu_custom_call" | custom-call | flops 10000000000 | bytes 1000000 | tf_op jit(solution)/shard_map/first_stats/pallas_call | solution.py:77
  31.9 2.0 %both_stats.1.refs_0_.refs_4_ = f32[16,1280]{1,0:T(8,128)S(1)} custom-call(bf16[256,256]{1,0:T(8,128)(2,1)S(1)} %collective-permute-done.7.refs_0_, bf16[2560,256]{1,0:T(8,128)(2,1)S(1)} %get-tuple-element.29.refs_1_.refs_2_, bf16[2560,256]{1,0:T(8,128)(2,1)S(1)} %get-tuple-element.30.refs_2_.refs_3_, f32[8,1280]{1,0:T(8,128)S(1)} %stats.3.refs_3_, ...), custom_call_target="tpu_custom_call" | custom-call | flops 10000000000 | bytes 1000000 | tf_op jit(solution)/shard_map/both_stats/pallas_call | solution.py:77
  34.0 1.3 %collective-permute-done.8.refs_1_ = f32[16,1280]{1,0:T(8,128)S(1)} collective-permute-done((f32[16,1280]{1,0:T(8,128)S(1)}, f32[16,1280]{1,0:T(8,128)S(1)}, u32[]{:S(2)}, u32[]{:S(2)}) %collective-permute-start.8) | collective-permute-done | bytes 81952 | tf_op jit(solution)/shard_map/ppermute | solution.py:446
  35.3 1.8 %collective-permute-start.9 = (f32[16,1280]{1,0:T(8,128)S(1)}, f32[16,1280]{1,0:T(8,128)S(1)}, u32[]{:S(2)}, u32[]{:S(2)}) collective-permute-start(f32[16,1280]{1,0:T(8,128)S(1)} %merge.2.refs_0_), channel_id=1, source_target_pairs={{0,16},{1,17},{2,18},{3,19},{4,20},{5,21},{6,22},{7,23},{8,24},{9,... | collective-permute-start | bytes 245768 | tf_op jit(solution)/shard_map/ppermute | solution.py:446
  38.4 2.4 %collective-permute-start.11 = (bf16[256,384]{1,0:T(8,128)(2,1)S(1)}, bf16[256,384]{1,0:T(8,128)(2,1)S(1)}, u32[]{:S(2)}, u32[]{:S(2)}) collective-permute-start(bf16[256,384]{1,0:T(8,128)(2,1)S(1)} %get-tuple-element.38), channel_id=1, source_target_pairs={{0,128},{32,160},{64,192},{96,224},{128,0},{160,32},{192,64},{224,... | collective-permute-start | bytes 589832 | tf_op jit(solution)/shard_map/ppermute | solution.py:440
  40.9 4.1 %scores.2 = (bf16[512,5120]{1,0:T(8,128)(2,1)S(1)}, bf16[512,5120]{1,0:T(8,128)(2,1)S(1)}, f32[128,2560]{1,0:T(8,128)S(1)}) custom-call(bf16[256,256]{1,0:T(8,128)(2,1)S(1)} %collective-permute-done.7.refs_0_, bf16[256,256]{1,0:T(8,128)(2,1)S(1)} %collective-permute-done.6.refs_4_.refs_0_.refs_1_, bf16[2560,256]{1,0:T(8,128)(2,1)S(1)} %get-tuple-element.29.refs_1_.refs_2_, ...), custom_call_target="tpu_custom_call" | custom-call | flops 1500000000 | bytes 1000000 | tf_op jit(solution)/shard_map/scores/pallas_call | solution.py:77
  45.1 2.9 %pair.3 = (bf16[256,256]{1,0:T(8,128)(2,1)S(1)}, bf16[256,256]{1,0:T(8,128)(2,1)S(1)}) custom-call(bf16[512,5120]{1,0:T(8,128)(2,1)S(1)} %get-tuple-element.34.refs_0_, bf16[512,5120]{1,0:T(8,128)(2,1)S(1)} %get-tuple-element.35.refs_1_, bf16[2560,256]{1,0:T(8,128)(2,1)S(1)} %get-tuple-element.29.refs_1_.refs_2_, ...), custom_call_target="tpu_custom_call" | custom-call | flops 1500000000 | bytes 1000000 | tf_op jit(solution)/shard_map/pair/pallas_call | solution.py:77
  48.8 1.8 %collective-permute-done.12.refs_9_.refs_4_ = bf16[256,384]{1,0:T(8,128)(2,1)S(1)} collective-permute-done((bf16[256,384]{1,0:T(8,128)(2,1)S(1)}, bf16[256,384]{1,0:T(8,128)(2,1)S(1)}, u32[]{:S(2)}, u32[]{:S(2)}) %collective-permute-start.12) | collective-permute-done | bytes 196640 | tf_op jit(solution)/shard_map/ppermute | solution.py:440
  50.5 4.2 %scores.3 = (bf16[512,5120]{1,0:T(8,128)(2,1)S(1)}, bf16[512,5120]{1,0:T(8,128)(2,1)S(1)}, f32[128,640]{1,0:T(8,128)S(1)}, bf16[128,640]{1,0:T(8,128)(2,1)S(1)},...) custom-call(bf16[256,256]{1,0:T(8,128)(2,1)S(1)} %collective-permute-done.2.refs_3_.refs_0_, ...), custom_call_target="tpu_custom_call" | custom-call | flops 1500000000 | bytes 1000000 | tf_op jit(solution)/shard_map/scores/pallas_call | solution.py:77
  56.9 1.8 %collective-permute-done.16.refs_4_.refs_1_ = bf16[256,256]{1,0:T(8,128)(2,1)S(1)} collective-permute-done((bf16[256,256]{1,0:T(8,128)(2,1)S(1)}, bf16[256,256]{1,0:T(8,128)(2,1)S(1)}, u32[]{:S(2)}, u32[]{:S(2)}) %collective-permute-start.16) | collective-permute-done | bytes 131104 | tf_op jit(solution)/shard_map/ppermute | solution.py:454
  58.8 1.5 %pair.4.refs_4_ = bf16[256,256]{1,0:T(8,128)(2,1)S(1)} custom-call(bf16[512,5120]{1,0:T(8,128)(2,1)S(1)} %get-tuple-element.44.refs_0_, bf16[512,5120]{1,0:T(8,128)(2,1)S(1)} %get-tuple-element.45.refs_1_, bf16[2560,256]{1,0:T(8,128)(2,1)S(1)} %get-tuple-element.29.refs_1_.refs_2_, bf16[2560,256]{1,0:T(8,128)(2,1)S(1)} %get-tuple-element.30.refs_2_.refs_3_, ...), custom_call_target="tpu_custom_call" | custom-call | flops 1500000000 | bytes 1000000 | tf_op jit(solution)/shard_map/pair/pallas_call | solution.py:77
  61.3 1.5 %pair.5.refs_4_.refs_0_ = f32[256,256]{1,0:T(8,128)S(1)} custom-call(bf16[512,5120]{1,0:T(8,128)(2,1)S(1)} %get-tuple-element.44.refs_0_, bf16[512,5120]{1,0:T(8,128)(2,1)S(1)} %get-tuple-element.45.refs_1_, bf16[2560,256]{1,0:T(8,128)(2,1)S(1)} %get-tuple-element.29.refs_1_.refs_2_, bf16[2560,256]{1,0:T(8,128)(2,1)S(1)} %get-tuple-element.30.refs_2_.refs_3_, ...), custom_call_target="tpu_custom_call" | custom-call | flops 1500000000 | bytes 1000000 | tf_op jit(solution)/shard_map/pair/pallas_call | solution.py:77
  62.9 1.2 %collective-permute-start.20 = (bf16[128,640]{1,0:T(8,128)(2,1)S(1)}, bf16[128,640]{1,0:T(8,128)(2,1)S(1)}, u32[]{:S(2)}, u32[]{:S(2)}) collective-permute-start(bf16[128,640]{1,0:T(8,128)(2,1)S(1)} %get-tuple-element.47.refs_5_.refs_0_), channel_id=1, source_target_pairs={{0,192},{32,224},{64,0},{96,32},{128,64},{160,96},{192,128},{224,1... | collective-permute-start | bytes 491528 | tf_op jit(solution)/shard_map/ppermute | solution.py:486
  64.1 2.2 %collective-permute-start.18 = (bf16[128,640]{1,0:T(8,128)(2,1)S(1)}, bf16[128,640]{1,0:T(8,128)(2,1)S(1)}, u32[]{:S(2)}, u32[]{:S(2)}) collective-permute-start(bf16[128,640]{1,0:T(8,128)(2,1)S(1)} %get-tuple-element.47.refs_5_.refs_0_), channel_id=1, source_target_pairs={{0,64},{32,96},{64,128},{96,160},{128,192},{160,224},{192,0},{224,... | collective-permute-start | bytes 491528 | tf_op jit(solution)/shard_map/ppermute | solution.py:485
  66.3 2.0 %collective-permute-start.19 = (bf16[128,256]{1,0:T(8,128)(2,1)S(1)}, bf16[128,256]{1,0:T(8,128)(2,1)S(1)}, u32[]{:S(2)}, u32[]{:S(2)}) collective-permute-start(bf16[128,256]{1,0:T(8,128)(2,1)S(1)} %get-tuple-element.48), channel_id=1, source_target_pairs={{0,128},{32,160},{64,192},{96,224},{128,0},{160,32},{192,64},{224,... | collective-permute-start | bytes 196616 | tf_op jit(solution)/shard_map/ppermute | solution.py:487
  69.1 1.2 %collective-permute-start.23 = (bf16[128,256]{1,0:T(8,128)(2,1)S(1)}, bf16[128,256]{1,0:T(8,128)(2,1)S(1)}, u32[]{:S(2)}, u32[]{:S(2)}) collective-permute-start(bf16[128,256]{1,0:T(8,128)(2,1)S(1)} %get-tuple-element.50), channel_id=1, source_target_pairs={{15,0},{0,1},{1,2},{2,3},{3,4},{4,5},{5,6},{6,7},{7,8},{8,9},{9,10... | collective-permute-start | bytes 196616 | tf_op jit(solution)/shard_map/ppermute | solution.py:468
  71.8 2.4 %collective-permute-done.23.refs_1_ = bf16[128,256]{1,0:T(8,128)(2,1)S(1)} collective-permute-done((bf16[128,256]{1,0:T(8,128)(2,1)S(1)}, bf16[128,256]{1,0:T(8,128)(2,1)S(1)}, u32[]{:S(2)}, u32[]{:S(2)}) %collective-permute-start.23) | collective-permute-done | bytes 65568 | tf_op jit(solution)/shard_map/ppermute | solution.py:468
  74.3 1.6 %collective-permute-start.24 = (bf16[128,256]{1,0:T(8,128)(2,1)S(1)}, bf16[128,256]{1,0:T(8,128)(2,1)S(1)}, u32[]{:S(2)}, u32[]{:S(2)}) collective-permute-start(bf16[128,256]{1,0:T(8,128)(2,1)S(1)} %piece_sum.1.refs_4_), channel_id=1, source_target_pairs={{0,64},{32,96},{64,128},{96,160},{128,192},{160,224},{192,0},{224,... | collective-permute-start | bytes 196616 | tf_op jit(solution)/shard_map/ppermute | solution.py:379
  75.9 1.8 %collective-permute-start.25 = (bf16[128,256]{1,0:T(8,128)(2,1)S(1)}, bf16[128,256]{1,0:T(8,128)(2,1)S(1)}, u32[]{:S(2)}, u32[]{:S(2)}) collective-permute-start(bf16[128,256]{1,0:T(8,128)(2,1)S(1)} %piece_sum.1.refs_4_), channel_id=1, source_target_pairs={{0,128},{32,160},{64,192},{96,224},{128,0},{160,32},{192,64},{224,... | collective-permute-start | bytes 196616 | tf_op jit(solution)/shard_map/ppermute | solution.py:379
  77.7 1.3 %collective-permute-start.26 = (bf16[128,256]{1,0:T(8,128)(2,1)S(1)}, bf16[128,256]{1,0:T(8,128)(2,1)S(1)}, u32[]{:S(2)}, u32[]{:S(2)}) collective-permute-start(bf16[128,256]{1,0:T(8,128)(2,1)S(1)} %piece_sum.1.refs_4_), channel_id=1, source_target_pairs={{0,192},{32,224},{64,0},{96,32},{128,64},{160,96},{192,128},{224,1... | collective-permute-start | bytes 196616 | tf_op jit(solution)/shard_map/ppermute | solution.py:379
  79.4 2.4 %collective-permute-done.25.refs_6_ = bf16[128,256]{1,0:T(8,128)(2,1)S(1)} collective-permute-done((bf16[128,256]{1,0:T(8,128)(2,1)S(1)}, bf16[128,256]{1,0:T(8,128)(2,1)S(1)}, u32[]{:S(2)}, u32[]{:S(2)}) %collective-permute-start.25) | collective-permute-done | bytes 65568 | tf_op jit(solution)/shard_map/ppermute | solution.py:379
  81.8 1.4 %collective-permute-done.26.refs_7_ = bf16[128,256]{1,0:T(8,128)(2,1)S(1)} collective-permute-done((bf16[128,256]{1,0:T(8,128)(2,1)S(1)}, bf16[128,256]{1,0:T(8,128)(2,1)S(1)}, u32[]{:S(2)}, u32[]{:S(2)}) %collective-permute-start.26) | collective-permute-done | bytes 65568 | tf_op jit(solution)/shard_map/ppermute | solution.py:379
  83.6 3.2 %collective-permute-start.28 = (bf16[640,128]{1,0:T(8,128)(2,1)S(1)}, bf16[640,128]{1,0:T(8,128)(2,1)S(1)}, u32[]{:S(2)}, u32[]{:S(2)}) collective-permute-start(bf16[640,128]{1,0:T(8,128)(2,1)S(1)} %get-tuple-element.55), channel_id=1, source_target_pairs={{0,32},{32,0},{64,96},{96,64},{128,160},{160,128},{192,224},{224,1... | collective-permute-start | bytes 491528 | tf_op jit(solution)/shard_map/ppermute | solution.py:509
  86.8 3.7 %collective-permute-done.28.refs_1_ = bf16[640,128]{1,0:T(8,128)(2,1)S(1)} collective-permute-done((bf16[640,128]{1,0:T(8,128)(2,1)S(1)}, bf16[640,128]{1,0:T(8,128)(2,1)S(1)}, u32[]{:S(2)}, u32[]{:S(2)}) %collective-permute-start.28) | collective-permute-done | bytes 163872 | tf_op jit(solution)/shard_map/ppermute | solution.py:509
  (72 shorter events, 14.3 us)
Async XLA Ops:
  0.7 2.4 %copy-start.4 = (bf16[128,1024]{1,0:T(8,128)(2,1)S(1)}, bf16[128,1024]{1,0:T(8,128)(2,1)}, u32[]{:S(2)}) copy-start(bf16[128,1024]{1,0:T(8,128)(2,1)} %refs_5_.1) | copy-start | bytes 786436
  4.8 15.0 %collective-permute-start.3 = (bf16[640,256]{1,0:T(8,128)(2,1)S(1)}, bf16[640,256]{1,0:T(8,128)(2,1)S(1)}, u32[]{:S(2)}, u32[]{:S(2)}) collective-permute-start(bf16[640,256]{1,0:T(8,128)(2,1)S(1)} %qd.1.refs_0_), channel_id=1, source_target_pairs={{0,1},{1,0},{2,3},{3,2},{4,5},{5,4},{6,7},{7,6},{8,9},{9,8},{10,11... | collective-permute-start | bytes 983048 | tf_op jit(solution)/shard_map/ppermute | solution.py:412
  4.9 10.2 %collective-permute-start = (bf16[128,256]{1,0:T(8,128)(2,1)S(1)}, bf16[128,256]{1,0:T(8,128)(2,1)S(1)}, u32[]{:S(2)}, u32[]{:S(2)}) collective-permute-start(bf16[128,256]{1,0:T(8,128)(2,1)S(1)} %copy-done.9), channel_id=1, source_target_pairs={{0,0},{1,15},{2,2},{3,1},{4,4},{5,3},{6,6},{7,5},{8,8},{9,7},{10,1... | collective-permute-start | bytes 196616 | tf_op jit(solution)/shard_map/ppermute | solution.py:402
  5.6 9.8 %collective-permute-start.1 = (bf16[128,256]{1,0:T(8,128)(2,1)S(1)}, bf16[128,256]{1,0:T(8,128)(2,1)S(1)}, u32[]{:S(2)}, u32[]{:S(2)}) collective-permute-start(bf16[128,256]{1,0:T(8,128)(2,1)S(1)} %copy-done.9), channel_id=1, source_target_pairs={{0,15},{1,0},{2,1},{3,2},{4,3},{5,4},{6,5},{7,6},{8,7},{9,8},{10,9... | collective-permute-start | bytes 196616 | tf_op jit(solution)/shard_map/ppermute | solution.py:402
  13.5 9.1 %collective-permute-start.4 = (bf16[640,256]{1,0:T(8,128)(2,1)S(1)}, bf16[640,256]{1,0:T(8,128)(2,1)S(1)}, u32[]{:S(2)}, u32[]{:S(2)}) collective-permute-start(bf16[640,256]{1,0:T(8,128)(2,1)S(1)} %qd.1.refs_0_), channel_id=1, source_target_pairs={{0,16},{1,17},{2,18},{3,19},{4,20},{5,21},{6,22},{7,23},{8,24},{9,... | collective-permute-start | bytes 983048 | tf_op jit(solution)/shard_map/ppermute | solution.py:413
  15.4 7.2 %collective-permute-start.2 = (bf16[256,256]{1,0:T(8,128)(2,1)S(1)}, bf16[256,256]{1,0:T(8,128)(2,1)S(1)}, u32[]{:S(2)}, u32[]{:S(2)}) collective-permute-start(bf16[256,256]{1,0:T(8,128)(2,1)S(1)} %constant_dynamic-update-slice_fusion.refs_2_.refs_1_), channel_id=1, source_target_pairs={{0,2},{1,15},{2,4},{3,1},{4,6},{5,3},{6,8},{7,5},{8,10},{9,7},{10,... | collective-permute-start | bytes 393224 | tf_op jit(solution)/shard_map/ppermute | solution.py:403
  16.4 11.0 %collective-permute-start.6 = (bf16[256,256]{1,0:T(8,128)(2,1)S(1)}, bf16[256,256]{1,0:T(8,128)(2,1)S(1)}, u32[]{:S(2)}, u32[]{:S(2)}) collective-permute-start(bf16[256,256]{1,0:T(8,128)(2,1)S(1)} %constant_dynamic-update-slice_fusion.refs_2_.refs_1_), channel_id=1, source_target_pairs={{0,4},{1,13},{2,6},{3,15},{4,8},{5,1},{6,10},{7,3},{8,12},{9,5},{1... | collective-permute-start | bytes 393224 | tf_op jit(solution)/shard_map/ppermute | solution.py:403
  16.4 15.4 %collective-permute-start.7 = (bf16[256,256]{1,0:T(8,128)(2,1)S(1)}, bf16[256,256]{1,0:T(8,128)(2,1)S(1)}, u32[]{:S(2)}, u32[]{:S(2)}) collective-permute-start(bf16[256,256]{1,0:T(8,128)(2,1)S(1)} %constant_dynamic-update-slice_fusion.refs_2_.refs_1_), channel_id=1, source_target_pairs={{0,6},{1,11},{2,8},{3,13},{4,10},{5,15},{6,12},{7,1},{8,14},{9,3},... | collective-permute-start | bytes 393224 | tf_op jit(solution)/shard_map/ppermute | solution.py:403
  22.6 6.0 %collective-permute-start.5 = (bf16[640,256]{1,0:T(8,128)(2,1)S(1)}, bf16[640,256]{1,0:T(8,128)(2,1)S(1)}, u32[]{:S(2)}, u32[]{:S(2)}) collective-permute-start(bf16[640,256]{1,0:T(8,128)(2,1)S(1)} %collective-permute-done.4.refs_0_), channel_id=1, source_target_pairs={{0,1},{1,0},{2,3},{3,2},{4,5},{5,4},{6,7},{7,6},{8,9},{9,8},{10,11... | collective-permute-start | bytes 983048 | tf_op jit(solution)/shard_map/ppermute | solution.py:414
  33.9 3.3 %copy-start.5 = (bf16[1024,128]{1,0:T(8,128)(2,1)S(1)}, bf16[1024,128]{1,0:T(8,128)(2,1)}, u32[]{:S(2)}) copy-start(bf16[1024,128]{1,0:T(8,128)(2,1)} %refs_2_.5) | copy-start | bytes 786436
  33.9 3.3 %copy-start.6 = (bf16[1024,128]{1,0:T(8,128)(2,1)S(1)}, bf16[1024,128]{1,0:T(8,128)(2,1)}, u32[]{:S(2)}) copy-start(bf16[1024,128]{1,0:T(8,128)(2,1)} %refs_3_.3) | copy-start | bytes 786436
  33.9 1.4 %collective-permute-start.8 = (f32[16,1280]{1,0:T(8,128)S(1)}, f32[16,1280]{1,0:T(8,128)S(1)}, u32[]{:S(2)}, u32[]{:S(2)}) collective-permute-start(f32[16,1280]{1,0:T(8,128)S(1)} %both_stats.1.refs_0_.refs_4_), channel_id=1, source_target_pairs={{0,1},{1,0},{2,3},{3,2},{4,5},{5,4},{6,7},{7,6},{8,9},{9,8},{10,11... | collective-permute-start | bytes 245768 | tf_op jit(solution)/shard_map/ppermute | solution.py:446
  35.3 5.5 %collective-permute-start.9 = (f32[16,1280]{1,0:T(8,128)S(1)}, f32[16,1280]{1,0:T(8,128)S(1)}, u32[]{:S(2)}, u32[]{:S(2)}) collective-permute-start(f32[16,1280]{1,0:T(8,128)S(1)} %merge.2.refs_0_), channel_id=1, source_target_pairs={{0,16},{1,17},{2,18},{3,19},{4,20},{5,21},{6,22},{7,23},{8,24},{9,... | collective-permute-start | bytes 245768 | tf_op jit(solution)/shard_map/ppermute | solution.py:446
  37.9 10.9 %collective-permute-start.10 = (bf16[256,384]{1,0:T(8,128)(2,1)S(1)}, bf16[256,384]{1,0:T(8,128)(2,1)S(1)}, u32[]{:S(2)}, u32[]{:S(2)}) collective-permute-start(bf16[256,384]{1,0:T(8,128)(2,1)S(1)} %get-tuple-element.37), channel_id=1, source_target_pairs={{0,64},{32,96},{64,128},{96,160},{128,192},{160,224},{192,0},{224,... | collective-permute-start | bytes 589832 | tf_op jit(solution)/shard_map/ppermute | solution.py:440
  38.4 10.4 %collective-permute-start.11 = (bf16[256,384]{1,0:T(8,128)(2,1)S(1)}, bf16[256,384]{1,0:T(8,128)(2,1)S(1)}, u32[]{:S(2)}, u32[]{:S(2)}) collective-permute-start(bf16[256,384]{1,0:T(8,128)(2,1)S(1)} %get-tuple-element.38), channel_id=1, source_target_pairs={{0,128},{32,160},{64,192},{96,224},{128,0},{160,32},{192,64},{224,... | collective-permute-start | bytes 589832 | tf_op jit(solution)/shard_map/ppermute | solution.py:440
  40.9 9.7 %collective-permute-start.12 = (bf16[256,384]{1,0:T(8,128)(2,1)S(1)}, bf16[256,384]{1,0:T(8,128)(2,1)S(1)}, u32[]{:S(2)}, u32[]{:S(2)}) collective-permute-start(bf16[256,384]{1,0:T(8,128)(2,1)S(1)} %get-tuple-element.39), channel_id=1, source_target_pairs={{0,192},{32,224},{64,0},{96,32},{128,64},{160,96},{192,128},{224,1... | collective-permute-start | bytes 589832 | tf_op jit(solution)/shard_map/ppermute | solution.py:440
  47.9 10.8 %collective-permute-start.16 = (bf16[256,256]{1,0:T(8,128)(2,1)S(1)}, bf16[256,256]{1,0:T(8,128)(2,1)S(1)}, u32[]{:S(2)}, u32[]{:S(2)}) collective-permute-start(bf16[256,256]{1,0:T(8,128)(2,1)S(1)} %get-tuple-element.36.refs_6_), channel_id=1, source_target_pairs={{6,0},{11,1},{8,2},{13,3},{10,4},{15,5},{12,6},{1,7},{14,8},{3,9},... | collective-permute-start | bytes 393224 | tf_op jit(solution)/shard_map/ppermute | solution.py:454
  48.0 10.8 %collective-permute-start.17 = (bf16[256,256]{1,0:T(8,128)(2,1)S(1)}, bf16[256,256]{1,0:T(8,128)(2,1)S(1)}, u32[]{:S(2)}, u32[]{:S(2)}) collective-permute-start(bf16[256,256]{1,0:T(8,128)(2,1)S(1)} %get-tuple-element.46), channel_id=1, source_target_pairs={{4,0},{13,1},{6,2},{15,3},{8,4},{1,5},{10,6},{3,7},{12,8},{5,9},{1... | collective-permute-start | bytes 393224 | tf_op jit(solution)/shard_map/ppermute | solution.py:454
  54.7 8.1 %collective-permute-start.13 = (bf16[128,640]{1,0:T(8,128)(2,1)S(1)}, bf16[128,640]{1,0:T(8,128)(2,1)S(1)}, u32[]{:S(2)}, u32[]{:S(2)}) collective-permute-start(bf16[128,640]{1,0:T(8,128)(2,1)S(1)} %get-tuple-element.41), channel_id=1, source_target_pairs={{0,16},{1,17},{2,18},{3,19},{4,20},{5,21},{6,22},{7,23},{8,24},{9,... | collective-permute-start | bytes 491528 | tf_op jit(solution)/shard_map/ppermute | solution.py:459
  55.2 7.6 %collective-permute-start.14 = (bf16[128,640]{1,0:T(8,128)(2,1)S(1)}, bf16[128,640]{1,0:T(8,128)(2,1)S(1)}, u32[]{:S(2)}, u32[]{:S(2)}) collective-permute-start(bf16[128,640]{1,0:T(8,128)(2,1)S(1)} %get-tuple-element.42), channel_id=1, source_target_pairs={{0,17},{1,16},{2,19},{3,18},{4,21},{5,20},{6,23},{7,22},{8,25},{9,... | collective-permute-start | bytes 491528 | tf_op jit(solution)/shard_map/ppermute | solution.py:459
  55.8 7.0 %collective-permute-start.15 = (bf16[128,640]{1,0:T(8,128)(2,1)S(1)}, bf16[128,640]{1,0:T(8,128)(2,1)S(1)}, u32[]{:S(2)}, u32[]{:S(2)}) collective-permute-start(bf16[128,640]{1,0:T(8,128)(2,1)S(1)} %get-tuple-element.43), channel_id=1, source_target_pairs={{0,1},{1,0},{2,3},{3,2},{4,5},{5,4},{6,7},{7,6},{8,9},{9,8},{10,11... | collective-permute-start | bytes 491528 | tf_op jit(solution)/shard_map/ppermute | solution.py:459
  60.3 8.0 %collective-permute-start.21 = (bf16[256,256]{1,0:T(8,128)(2,1)S(1)}, bf16[256,256]{1,0:T(8,128)(2,1)S(1)}, u32[]{:S(2)}, u32[]{:S(2)}) collective-permute-start(bf16[256,256]{1,0:T(8,128)(2,1)S(1)} %pair.4.refs_4_), channel_id=1, source_target_pairs={{2,0},{15,1},{4,2},{1,3},{6,4},{3,5},{8,6},{5,7},{10,8},{7,9},{12,... | collective-permute-start | bytes 393224 | tf_op jit(solution)/shard_map/ppermute | solution.py:463
  62.9 8.0 %collective-permute-start.20 = (bf16[128,640]{1,0:T(8,128)(2,1)S(1)}, bf16[128,640]{1,0:T(8,128)(2,1)S(1)}, u32[]{:S(2)}, u32[]{:S(2)}) collective-permute-start(bf16[128,640]{1,0:T(8,128)(2,1)S(1)} %get-tuple-element.47.refs_5_.refs_0_), channel_id=1, source_target_pairs={{0,192},{32,224},{64,0},{96,32},{128,64},{160,96},{192,128},{224,1... | collective-permute-start | bytes 491528 | tf_op jit(solution)/shard_map/ppermute | solution.py:486
  64.1 14.9 %collective-permute-start.18 = (bf16[128,640]{1,0:T(8,128)(2,1)S(1)}, bf16[128,640]{1,0:T(8,128)(2,1)S(1)}, u32[]{:S(2)}, u32[]{:S(2)}) collective-permute-start(bf16[128,640]{1,0:T(8,128)(2,1)S(1)} %get-tuple-element.47.refs_5_.refs_0_), channel_id=1, source_target_pairs={{0,64},{32,96},{64,128},{96,160},{128,192},{160,224},{192,0},{224,... | collective-permute-start | bytes 491528 | tf_op jit(solution)/shard_map/ppermute | solution.py:485
  66.3 11.4 %collective-permute-start.19 = (bf16[128,256]{1,0:T(8,128)(2,1)S(1)}, bf16[128,256]{1,0:T(8,128)(2,1)S(1)}, u32[]{:S(2)}, u32[]{:S(2)}) collective-permute-start(bf16[128,256]{1,0:T(8,128)(2,1)S(1)} %get-tuple-element.48), channel_id=1, source_target_pairs={{0,128},{32,160},{64,192},{96,224},{128,0},{160,32},{192,64},{224,... | collective-permute-start | bytes 196616 | tf_op jit(solution)/shard_map/ppermute | solution.py:487
  68.4 3.4 %collective-permute-start.22 = (bf16[128,256]{1,0:T(8,128)(2,1)S(1)}, bf16[128,256]{1,0:T(8,128)(2,1)S(1)}, u32[]{:S(2)}, u32[]{:S(2)}) collective-permute-start(bf16[128,256]{1,0:T(8,128)(2,1)S(1)} %get-tuple-element.49), channel_id=1, source_target_pairs={{0,0},{15,1},{2,2},{1,3},{4,4},{3,5},{6,6},{5,7},{8,8},{7,9},{10,1... | collective-permute-start | bytes 196616 | tf_op jit(solution)/shard_map/ppermute | solution.py:468
  69.1 5.2 %collective-permute-start.23 = (bf16[128,256]{1,0:T(8,128)(2,1)S(1)}, bf16[128,256]{1,0:T(8,128)(2,1)S(1)}, u32[]{:S(2)}, u32[]{:S(2)}) collective-permute-start(bf16[128,256]{1,0:T(8,128)(2,1)S(1)} %get-tuple-element.50), channel_id=1, source_target_pairs={{15,0},{0,1},{1,2},{2,3},{3,4},{4,5},{5,6},{6,7},{7,8},{8,9},{9,10... | collective-permute-start | bytes 196616 | tf_op jit(solution)/shard_map/ppermute | solution.py:468
  71.0 8.1 %collective-permute-start.27 = (bf16[128,384]{1,0:T(8,128)(2,1)S(1)}, bf16[128,384]{1,0:T(8,128)(2,1)S(1)}, u32[]{:S(2)}, u32[]{:S(2)}) collective-permute-start(bf16[128,384]{1,0:T(8,128)(2,1)S(1)} %slice.4), channel_id=1, source_target_pairs={{0,192},{32,224},{64,0},{96,32},{128,64},{160,96},{192,128},{224,1... | collective-permute-start | bytes 294920 | tf_op jit(solution)/shard_map/ppermute | solution.py:488
  74.3 5.1 %collective-permute-start.24 = (bf16[128,256]{1,0:T(8,128)(2,1)S(1)}, bf16[128,256]{1,0:T(8,128)(2,1)S(1)}, u32[]{:S(2)}, u32[]{:S(2)}) collective-permute-start(bf16[128,256]{1,0:T(8,128)(2,1)S(1)} %piece_sum.1.refs_4_), channel_id=1, source_target_pairs={{0,64},{32,96},{64,128},{96,160},{128,192},{160,224},{192,0},{224,... | collective-permute-start | bytes 196616 | tf_op jit(solution)/shard_map/ppermute | solution.py:379
  75.9 5.9 %collective-permute-start.25 = (bf16[128,256]{1,0:T(8,128)(2,1)S(1)}, bf16[128,256]{1,0:T(8,128)(2,1)S(1)}, u32[]{:S(2)}, u32[]{:S(2)}) collective-permute-start(bf16[128,256]{1,0:T(8,128)(2,1)S(1)} %piece_sum.1.refs_4_), channel_id=1, source_target_pairs={{0,128},{32,160},{64,192},{96,224},{128,0},{160,32},{192,64},{224,... | collective-permute-start | bytes 196616 | tf_op jit(solution)/shard_map/ppermute | solution.py:379
  77.7 5.5 %collective-permute-start.26 = (bf16[128,256]{1,0:T(8,128)(2,1)S(1)}, bf16[128,256]{1,0:T(8,128)(2,1)S(1)}, u32[]{:S(2)}, u32[]{:S(2)}) collective-permute-start(bf16[128,256]{1,0:T(8,128)(2,1)S(1)} %piece_sum.1.refs_4_), channel_id=1, source_target_pairs={{0,192},{32,224},{64,0},{96,32},{128,64},{160,96},{192,128},{224,1... | collective-permute-start | bytes 196616 | tf_op jit(solution)/shard_map/ppermute | solution.py:379
  83.6 6.9 %collective-permute-start.28 = (bf16[640,128]{1,0:T(8,128)(2,1)S(1)}, bf16[640,128]{1,0:T(8,128)(2,1)S(1)}, u32[]{:S(2)}, u32[]{:S(2)}) collective-permute-start(bf16[640,128]{1,0:T(8,128)(2,1)S(1)} %get-tuple-element.55), channel_id=1, source_target_pairs={{0,32},{32,0},{64,96},{96,64},{128,160},{160,128},{192,224},{224,1... | collective-permute-start | bytes 491528 | tf_op jit(solution)/shard_map/ppermute | solution.py:509
  (7 other events, 13.5 us)

commit v2 on v1

--- a/solution.py
+++ b/solution.py
@@ -428,16 +428,20 @@
         (stats_a,) = call(
             next_stats_kernel, [sds((8, total), F32)], [blocks[j], rhs_a, stats_a], "stats"
         )
+        if j == 1:
+            own_weights, part = weight_rows((0, 1), [stats_a])
+            x_weights = [own_weights, lax.ppermute(part, HEAD, SHIFT_X[1])]
     stats_b, rhs_b = first_stats(y_rows, both_rows, blocks[:HOPS])
     (stats,) = call(
         both_stats_kernel,
         [sds((16, total), F32)],
         [blocks[HOPS], rhs_a, rhs_b, stats_a, stats_b],
         "both_stats",
-    )
-    x_weights = weight_rows(tuple(range(X)), [stats])
-    x_weights = [x_weights[0]] + [
-        lax.ppermute(x_weights[r], HEAD, SHIFT_X[r]) for r in range(1, X)
+        after=x_weights[1:],
+    )
+    x_weights += [
+        lax.ppermute(part, HEAD, SHIFT_X[r])
+        for r, part in zip((2, 3), weight_rows((2, 3), [stats]))
     ]
     for merge_kernel, perm in ((merge_cores_kernel, SWAP_CORE), (merge_y_kernel, SWAP_Y)):
         (stats,) = call(
@@ -459,13 +463,9 @@
         lax.ppermute(part, TOK, perm)
         for part, perm in ((dq_y, SWAP_Y), (dq_both, SWAP_BOTH), (dq_core, SWAP_CORE))
     ]
-    (dkv_1,) = pair(weights, rhs, 0, [sds((n, 256), BF16)], after=list(sums))
+    (dkv_1,) = pair(weights, rhs, 0, [sds((n, 256), BF16)])
     sums.append(lax.ppermute(dkv_1, TOK, BACK[1]))
-    (dkv,) = pair(weights, rhs, n, [sds((n, 256), F32)], after=[dkv_1])
-    pieces = call(
-        pair_sum_kernel, [sds((na, 256), BF16)] * len(RETURN), [dkv, *sums], "pair_sum"
-    )
-    pieces = [lax.ppermute(piece, TOK, perm) for piece, perm in zip(pieces, RETURN)]
+    (dkv,) = pair(weights, rhs, n, [sds((n, 256), F32)], after=[dkv_1, *sums[:2]])
     cut = 2 * 128
     dq, dq_first = call(
         dq_sum_kernel,
@@ -474,6 +474,10 @@
         "dq_sum",
         after=[dkv],
     )
+    pieces = call(
+        pair_sum_kernel, [sds((na, 256), BF16)] * len(RETURN), [dkv, *sums], "pair_sum", after=[dq]
+    )
+    pieces = [lax.ppermute(piece, TOK, perm) for piece, perm in zip(pieces, RETURN)]
     (x_weights,) = call(
         stack_kernel,
         [sds((256, X * 384), BF16)],

time: 91.4 us -> 90.9 us (level)
  starting transfers between devices: 39.7 us -> 38.7 us
    ppermute x3, waiting for transfers between devices: 0.01 us -> 1.92 us  [per_device(): lax.ppermute(part, TOK, perm)]
    ppermute x1, waiting for transfers between devices: 1.84 us -> 0.01 us  [per_device(): lax.ppermute(dkv_3, TOK, BACK[3])]
    ppermute x1, starting transfers between devices: 2.02 us -> 0.19 us  [per_device(): back_2a = lax.ppermute(dq_first, HEAD, SHIFT_X[2])]
    ppermute x1, starting transfers between devices: 0.76 us -> 2.58 us  [per_device(): lax.ppermute(dkv_2, TOK, BACK[2])]
    ppermute x3, waiting for transfers between devices: 1.76 us -> 0.01 us  [the longest x2 0.01 us: per_device(): lax.ppermute(part, HEAD, SHIFT_X[r])]
    ppermute x1, waiting for transfers between devices: 1.56 us -> 0.01 us  [per_device(): y_rows = lax.ppermute(mine, TOK, SWAP_Y)]
    ppermute x2, starting transfers between devices: 1.82 us -> 2.94 us  [per_device(): lax.ppermute(piece, TOK, perm)]
    ppermute x1, waiting for transfers between devices: 0.07 us -> 1.07 us  [per_device(): back_3 = lax.ppermute(dq, HEAD, SHIFT_X[3])]
  transfers between devices with their start and end apart: 29 -> 29, of which waited for: 11 -> 13; matrix products, arithmetic and copies ran while one was open for 0% -> 0% of each run, Pallas kernels for 25% -> 26%
where the time goes in v2:
time: 90.9 us; the launch traced here: 90.7 us
  starting transfers between devices  38.7 us (43%)
  Pallas kernels  29.5 us (32%)
  waiting for transfers between devices  20.7 us (23%)
  between operations  0.96 us (1%)
    pallas_call x23, Pallas kernels, call(): pl.pallas_call(kernel, out_shape=tuple(outs), in_specs=[spec(i) for i in...  29.5 us
    ppermute x2, starting transfers between devices, per_device(): lax.ppermute(kv, TOK, perm)  8.59 us
    ppermute x3, starting transfers between devices, per_device(): lax.ppermute(block, TOK, FORTH[j])  4.38 us
    ppermute x3, starting transfers between devices, over_x(): lax.ppermute(array, HEAD, SHIFT_X[r])  4.13 us
    ppermute x3, waiting for transfers between devices, per_device(): lax.ppermute(block, TOK, FORTH[j])  4.13 us
    ppermute x1, waiting for transfers between devices, per_device(): lax.ppermute(theirs, HEAD, SWAP_YH)  3.92 us
    ppermute x3, waiting for transfers between devices, over_x(): lax.ppermute(array, HEAD, SHIFT_X[r])  3.92 us
    ppermute x2, waiting for transfers between devices, per_device(): lax.ppermute(piece, TOK, perm)  3.33 us
  transfers between devices with their start and end apart: 29, of which 13 were waited for; matrix products, arithmetic and copies ran while one was open for 0% of the time, Pallas kernels for 26%

profile of v2, /device:TPU:6, one launch (start us, length us, event | category | flops | bytes accessed | tf_op | source)
XLA Modules:
  0.0 90.7 jit_solution(13257546445525259481)
XLA Ops:
  0.7 2.3 %kv.1.refs_7_ = bf16[128,256]{1,0:T(8,128)(2,1)} custom-call(bf16[128,1024]{1,0:T(8,128)(2,1)} %refs_0_.3, bf16[1024,128]{1,0:T(8,128)(2,1)} %refs_2_.7, bf16[1024,128]{1,0:T(8,128)(2,1)} %refs_3_.5), custom_call_target="tpu_custom_call" | custom-call | flops 10000000000 | bytes 1000000 | tf_op jit(solution)/shard_map/kv/pallas_call | solution.py:77
  5.5 7.9 %collective-permute-start.1 = (bf16[128,256]{1,0:T(8,128)(2,1)S(1)}, bf16[128,256]{1,0:T(8,128)(2,1)S(1)}, u32[]{:S(2)}, u32[]{:S(2)}) collective-permute-start(bf16[128,256]{1,0:T(8,128)(2,1)S(1)} %copy-done.8), channel_id=1, source_target_pairs={{0,15},{1,0},{2,1},{3,2},{4,3},{5,4},{6,5},{7,6},{8,7},{9,8},{10,9... | collective-permute-start | bytes 196616 | tf_op jit(solution)/shard_map/ppermute | solution.py:402
  13.5 1.6 %collective-permute-start.4 = (bf16[640,256]{1,0:T(8,128)(2,1)S(1)}, bf16[640,256]{1,0:T(8,128)(2,1)S(1)}, u32[]{:S(2)}, u32[]{:S(2)}) collective-permute-start(bf16[640,256]{1,0:T(8,128)(2,1)S(1)} %qd.1.refs_0_), channel_id=1, source_target_pairs={{0,16},{1,17},{2,18},{3,19},{4,20},{5,21},{6,22},{7,23},{8,24},{9,... | collective-permute-start | bytes 983048 | tf_op jit(solution)/shard_map/ppermute | solution.py:413
  15.4 1.0 %collective-permute-start.2 = (bf16[256,256]{1,0:T(8,128)(2,1)S(1)}, bf16[256,256]{1,0:T(8,128)(2,1)S(1)}, u32[]{:S(2)}, u32[]{:S(2)}) collective-permute-start(bf16[256,256]{1,0:T(8,128)(2,1)S(1)} %constant_dynamic-update-slice_fusion.refs_2_.refs_1_), channel_id=1, source_target_pairs={{0,2},{1,15},{2,4},{3,1},{4,6},{5,3},{6,8},{7,5},{8,10},{9,7},{10,... | collective-permute-start | bytes 393224 | tf_op jit(solution)/shard_map/ppermute | solution.py:403
  16.4 3.4 %collective-permute-start.7 = (bf16[256,256]{1,0:T(8,128)(2,1)S(1)}, bf16[256,256]{1,0:T(8,128)(2,1)S(1)}, u32[]{:S(2)}, u32[]{:S(2)}) collective-permute-start(bf16[256,256]{1,0:T(8,128)(2,1)S(1)} %constant_dynamic-update-slice_fusion.refs_2_.refs_1_), channel_id=1, source_target_pairs={{0,6},{1,11},{2,8},{3,13},{4,10},{5,15},{6,12},{7,1},{8,14},{9,3},... | collective-permute-start | bytes 393224 | tf_op jit(solution)/shard_map/ppermute | solution.py:403
  19.8 1.2 %first_stats.2 = (f32[8,1280]{1,0:T(8,128)S(1)}, bf16[2560,256]{1,0:T(8,128)(2,1)S(1)}) custom-call(bf16[640,256]{1,0:T(8,128)(2,1)S(1)} %qd.1.refs_0_, bf16[640,256]{1,0:T(8,128)(2,1)S(1)} %collective-permute-done.3.refs_1_, bf16[256,256]{1,0:T(8,128)(2,1)S(1)} %constant_dynamic-update-slice_fusion.refs_2_.refs_1_), custom_call_target="tpu_custom_call" | custom-call | flops 10000000000 | bytes 1000000 | tf_op jit(solution)/shard_map/first_stats/pallas_call | solution.py:77
  21.6 1.1 %stats.2.refs_2_.refs_4_ = f32[8,1280]{1,0:T(8,128)S(1)} custom-call(bf16[256,256]{1,0:T(8,128)(2,1)S(1)} %collective-permute-done.2.refs_3_.refs_0_, bf16[2560,256]{1,0:T(8,128)(2,1)S(1)} %get-tuple-element.29.refs_1_.refs_2_, f32[8,1280]{1,0:T(8,128)S(1)} %get-tuple-element.31.refs_2_), custom_call_target="tpu_custom_call" | custom-call | flops 10000000000 | bytes 1000000 | tf_op jit(solution)/shard_map/stats/pallas_call | solution.py:77
  23.8 3.5 %collective-permute-done.6.refs_4_.refs_0_.refs_1_ = bf16[256,256]{1,0:T(8,128)(2,1)S(1)} collective-permute-done((bf16[256,256]{1,0:T(8,128)(2,1)S(1)}, bf16[256,256]{1,0:T(8,128)(2,1)S(1)}, u32[]{:S(2)}, u32[]{:S(2)}) %collective-permute-start.6) | collective-permute-done | bytes 131104 | tf_op jit(solution)/shard_map/ppermute | solution.py:403
  27.4 1.1 %stats.3.refs_3_ = f32[8,1280]{1,0:T(8,128)S(1)} custom-call(bf16[256,256]{1,0:T(8,128)(2,1)S(1)} %collective-permute-done.6.refs_4_.refs_0_.refs_1_, bf16[2560,256]{1,0:T(8,128)(2,1)S(1)} %get-tuple-element.29.refs_1_.refs_2_, f32[8,1280]{1,0:T(8,128)S(1)} %stats.2.refs_2_.refs_4_), custom_call_target="tpu_custom_call" | custom-call | flops 10000000000 | bytes 1000000 | tf_op jit(solution)/shard_map/stats/pallas_call | solution.py:77
  28.5 3.3 %first_stats.3 = (f32[8,1280]{1,0:T(8,128)S(1)}, bf16[2560,256]{1,0:T(8,128)(2,1)S(1)}) custom-call(bf16[640,256]{1,0:T(8,128)(2,1)S(1)} %collective-permute-done.4.refs_0_, bf16[640,256]{1,0:T(8,128)(2,1)S(1)} %collective-permute-done.5.refs_1_, bf16[256,256]{1,0:T(8,128)(2,1)S(1)} %constant_dynamic-update-slice_fusion.refs_2_.refs_1_, ...), custom_call_target="tpu_custom_call" | custom-call | flops 10000000000 | bytes 1000000 | tf_op jit(solution)/shard_map/first_stats/pallas_call | solution.py:77
  31.8 2.0 %both_stats.1.refs_0_.refs_4_ = f32[16,1280]{1,0:T(8,128)S(1)} custom-call(bf16[256,256]{1,0:T(8,128)(2,1)S(1)} %collective-permute-done.7.refs_0_, bf16[2560,256]{1,0:T(8,128)(2,1)S(1)} %get-tuple-element.29.refs_1_.refs_2_, bf16[2560,256]{1,0:T(8,128)(2,1)S(1)} %get-tuple-element.30.refs_2_.refs_3_, f32[8,1280]{1,0:T(8,128)S(1)} %stats.3.refs_3_, ...), custom_call_target="tpu_custom_call" | custom-call | flops 10000000000 | bytes 1000000 | tf_op jit(solution)/shard_map/both_stats/pallas_call | solution.py:77
  33.9 1.3 %collective-permute-done.9.refs_1_ = f32[16,1280]{1,0:T(8,128)S(1)} collective-permute-done((f32[16,1280]{1,0:T(8,128)S(1)}, f32[16,1280]{1,0:T(8,128)S(1)}, u32[]{:S(2)}, u32[]{:S(2)}) %collective-permute-start.9) | collective-permute-done | bytes 81952 | tf_op jit(solution)/shard_map/ppermute | solution.py:450
  35.2 1.7 %collective-permute-start.10 = (f32[16,1280]{1,0:T(8,128)S(1)}, f32[16,1280]{1,0:T(8,128)S(1)}, u32[]{:S(2)}, u32[]{:S(2)}) collective-permute-start(f32[16,1280]{1,0:T(8,128)S(1)} %merge.2.refs_0_), channel_id=1, source_target_pairs={{0,16},{1,17},{2,18},{3,19},{4,20},{5,21},{6,22},{7,23},{8,24},{9,... | collective-permute-start | bytes 245768 | tf_op jit(solution)/shard_map/ppermute | solution.py:450
  37.5 1.5 %collective-permute-start.11 = (bf16[256,384]{1,0:T(8,128)(2,1)S(1)}, bf16[256,384]{1,0:T(8,128)(2,1)S(1)}, u32[]{:S(2)}, u32[]{:S(2)}) collective-permute-start(bf16[256,384]{1,0:T(8,128)(2,1)S(1)} %get-tuple-element.38), channel_id=1, source_target_pairs={{0,128},{32,160},{64,192},{96,224},{128,0},{160,32},{192,64},{224,... | collective-permute-start | bytes 589832 | tf_op jit(solution)/shard_map/ppermute | solution.py:443
  39.8 4.1 %scores.2 = (bf16[512,5120]{1,0:T(8,128)(2,1)S(1)}, bf16[512,5120]{1,0:T(8,128)(2,1)S(1)}, f32[128,2560]{1,0:T(8,128)S(1)}) custom-call(bf16[256,256]{1,0:T(8,128)(2,1)S(1)} %collective-permute-done.7.refs_0_, bf16[256,256]{1,0:T(8,128)(2,1)S(1)} %collective-permute-done.6.refs_4_.refs_0_.refs_1_, bf16[2560,256]{1,0:T(8,128)(2,1)S(1)} %get-tuple-element.29.refs_1_.refs_2_, ...), custom_call_target="tpu_custom_call" | custom-call | flops 1500000000 | bytes 1000000 | tf_op jit(solution)/shard_map/scores/pallas_call | solution.py:77
  44.0 2.9 %pair.3 = (bf16[256,256]{1,0:T(8,128)(2,1)S(1)}, bf16[256,256]{1,0:T(8,128)(2,1)S(1)}) custom-call(bf16[512,5120]{1,0:T(8,128)(2,1)S(1)} %get-tuple-element.35.refs_0_, bf16[512,5120]{1,0:T(8,128)(2,1)S(1)} %get-tuple-element.36.refs_1_, bf16[2560,256]{1,0:T(8,128)(2,1)S(1)} %get-tuple-element.29.refs_1_.refs_2_, ...), custom_call_target="tpu_custom_call" | custom-call | flops 1500000000 | bytes 1000000 | tf_op jit(solution)/shard_map/pair/pallas_call | solution.py:77
  47.7 2.6 %collective-permute-start.17 = (bf16[256,256]{1,0:T(8,128)(2,1)S(1)}, bf16[256,256]{1,0:T(8,128)(2,1)S(1)}, u32[]{:S(2)}, u32[]{:S(2)}) collective-permute-start(bf16[256,256]{1,0:T(8,128)(2,1)S(1)} %get-tuple-element.46), channel_id=1, source_target_pairs={{4,0},{13,1},{6,2},{15,3},{8,4},{1,5},{10,6},{3,7},{12,8},{5,9},{1... | collective-permute-start | bytes 393224 | tf_op jit(solution)/shard_map/ppermute | solution.py:458
  50.3 4.2 %scores.3 = (bf16[512,5120]{1,0:T(8,128)(2,1)S(1)}, bf16[512,5120]{1,0:T(8,128)(2,1)S(1)}, f32[128,640]{1,0:T(8,128)S(1)}, bf16[128,640]{1,0:T(8,128)(2,1)S(1)},...) custom-call(bf16[256,256]{1,0:T(8,128)(2,1)S(1)} %collective-permute-done.2.refs_3_.refs_0_, ...), custom_call_target="tpu_custom_call" | custom-call | flops 1500000000 | bytes 1000000 | tf_op jit(solution)/shard_map/scores/pallas_call | solution.py:77
  54.4 1.3 %collective-permute-start.13 = (bf16[128,640]{1,0:T(8,128)(2,1)S(1)}, bf16[128,640]{1,0:T(8,128)(2,1)S(1)}, u32[]{:S(2)}, u32[]{:S(2)}) collective-permute-start(bf16[128,640]{1,0:T(8,128)(2,1)S(1)} %get-tuple-element.41), channel_id=1, source_target_pairs={{0,16},{1,17},{2,18},{3,19},{4,20},{5,21},{6,22},{7,23},{8,24},{9,... | collective-permute-start | bytes 491528 | tf_op jit(solution)/shard_map/ppermute | solution.py:463
  56.7 1.5 %pair.4.refs_4_ = bf16[256,256]{1,0:T(8,128)(2,1)S(1)} custom-call(bf16[512,5120]{1,0:T(8,128)(2,1)S(1)} %get-tuple-element.44.refs_0_, bf16[512,5120]{1,0:T(8,128)(2,1)S(1)} %get-tuple-element.45.refs_1_, bf16[2560,256]{1,0:T(8,128)(2,1)S(1)} %get-tuple-element.29.refs_1_.refs_2_, bf16[2560,256]{1,0:T(8,128)(2,1)S(1)} %get-tuple-element.30.refs_2_.refs_3_), custom_call_target="tpu_custom_call" | custom-call | flops 1500000000 | bytes 1000000 | tf_op jit(solution)/shard_map/pair/pallas_call | solution.py:77
  59.1 1.5 %pair.5.refs_4_.refs_0_ = f32[256,256]{1,0:T(8,128)S(1)} custom-call(bf16[512,5120]{1,0:T(8,128)(2,1)S(1)} %get-tuple-element.44.refs_0_, bf16[512,5120]{1,0:T(8,128)(2,1)S(1)} %get-tuple-element.45.refs_1_, bf16[2560,256]{1,0:T(8,128)(2,1)S(1)} %get-tuple-element.29.refs_1_.refs_2_, bf16[2560,256]{1,0:T(8,128)(2,1)S(1)} %get-tuple-element.30.refs_2_.refs_3_, ...), custom_call_target="tpu_custom_call" | custom-call | flops 1500000000 | bytes 1000000 | tf_op jit(solution)/shard_map/pair/pallas_call | solution.py:77
  63.2 2.8 %collective-permute-start.18 = (bf16[128,640]{1,0:T(8,128)(2,1)S(1)}, bf16[128,640]{1,0:T(8,128)(2,1)S(1)}, u32[]{:S(2)}, u32[]{:S(2)}) collective-permute-start(bf16[128,640]{1,0:T(8,128)(2,1)S(1)} %get-tuple-element.47.refs_4_.refs_5_.refs_0_), channel_id=1, source_target_pairs={{0,64},{32,96},{64,128},{96,160},{128,192},{160,224},{192,0},{224,... | collective-permute-start | bytes 491528 | tf_op jit(solution)/shard_map/ppermute | solution.py:489
  66.9 2.3 %collective-permute-start.23 = (bf16[128,256]{1,0:T(8,128)(2,1)S(1)}, bf16[128,256]{1,0:T(8,128)(2,1)S(1)}, u32[]{:S(2)}, u32[]{:S(2)}) collective-permute-start(bf16[128,256]{1,0:T(8,128)(2,1)S(1)} %get-tuple-element.50), channel_id=1, source_target_pairs={{15,0},{0,1},{1,2},{2,3},{3,4},{4,5},{5,6},{6,7},{7,8},{8,9},{9,10... | collective-permute-start | bytes 196616 | tf_op jit(solution)/shard_map/ppermute | solution.py:480
  69.8 1.1 %collective-permute-done.20.refs_4_.refs_3_ = bf16[128,640]{1,0:T(8,128)(2,1)S(1)} collective-permute-done((bf16[128,640]{1,0:T(8,128)(2,1)S(1)}, bf16[128,640]{1,0:T(8,128)(2,1)S(1)}, u32[]{:S(2)}, u32[]{:S(2)}) %collective-permute-start.20) | collective-permute-done | bytes 163872 | tf_op jit(solution)/shard_map/ppermute | solution.py:490
  71.0 3.3 %collective-permute-done.23.refs_1_ = bf16[128,256]{1,0:T(8,128)(2,1)S(1)} collective-permute-done((bf16[128,256]{1,0:T(8,128)(2,1)S(1)}, bf16[128,256]{1,0:T(8,128)(2,1)S(1)}, u32[]{:S(2)}, u32[]{:S(2)}) %collective-permute-start.23) | collective-permute-done | bytes 65568 | tf_op jit(solution)/shard_map/ppermute | solution.py:480
  74.3 1.3 %collective-permute-start.24 = (bf16[128,256]{1,0:T(8,128)(2,1)S(1)}, bf16[128,256]{1,0:T(8,128)(2,1)S(1)}, u32[]{:S(2)}, u32[]{:S(2)}) collective-permute-start(bf16[128,256]{1,0:T(8,128)(2,1)S(1)} %piece_sum.1.refs_4_), channel_id=1, source_target_pairs={{0,64},{32,96},{64,128},{96,160},{128,192},{160,224},{192,0},{224,... | collective-permute-start | bytes 196616 | tf_op jit(solution)/shard_map/ppermute | solution.py:379
  75.6 1.7 %collective-permute-start.25 = (bf16[128,256]{1,0:T(8,128)(2,1)S(1)}, bf16[128,256]{1,0:T(8,128)(2,1)S(1)}, u32[]{:S(2)}, u32[]{:S(2)}) collective-permute-start(bf16[128,256]{1,0:T(8,128)(2,1)S(1)} %piece_sum.1.refs_4_), channel_id=1, source_target_pairs={{0,128},{32,160},{64,192},{96,224},{128,0},{160,32},{192,64},{224,... | collective-permute-start | bytes 196616 | tf_op jit(solution)/shard_map/ppermute | solution.py:379
  77.3 1.2 %collective-permute-start.26 = (bf16[128,256]{1,0:T(8,128)(2,1)S(1)}, bf16[128,256]{1,0:T(8,128)(2,1)S(1)}, u32[]{:S(2)}, u32[]{:S(2)}) collective-permute-start(bf16[128,256]{1,0:T(8,128)(2,1)S(1)} %piece_sum.1.refs_4_), channel_id=1, source_target_pairs={{0,192},{32,224},{64,0},{96,32},{128,64},{160,96},{192,128},{224,1... | collective-permute-start | bytes 196616 | tf_op jit(solution)/shard_map/ppermute | solution.py:379
  79.3 2.2 %collective-permute-done.25.refs_6_ = bf16[128,256]{1,0:T(8,128)(2,1)S(1)} collective-permute-done((bf16[128,256]{1,0:T(8,128)(2,1)S(1)}, bf16[128,256]{1,0:T(8,128)(2,1)S(1)}, u32[]{:S(2)}, u32[]{:S(2)}) %collective-permute-start.25) | collective-permute-done | bytes 65568 | tf_op jit(solution)/shard_map/ppermute | solution.py:379
  81.4 1.3 %collective-permute-done.26.refs_7_ = bf16[128,256]{1,0:T(8,128)(2,1)S(1)} collective-permute-done((bf16[128,256]{1,0:T(8,128)(2,1)S(1)}, bf16[128,256]{1,0:T(8,128)(2,1)S(1)}, u32[]{:S(2)}, u32[]{:S(2)}) %collective-permute-start.26) | collective-permute-done | bytes 65568 | tf_op jit(solution)/shard_map/ppermute | solution.py:379
  83.2 3.0 %collective-permute-start.28 = (bf16[640,128]{1,0:T(8,128)(2,1)S(1)}, bf16[640,128]{1,0:T(8,128)(2,1)S(1)}, u32[]{:S(2)}, u32[]{:S(2)}) collective-permute-start(bf16[640,128]{1,0:T(8,128)(2,1)S(1)} %get-tuple-element.55), channel_id=1, source_target_pairs={{0,32},{32,0},{64,96},{96,64},{128,160},{160,128},{192,224},{224,1... | collective-permute-start | bytes 491528 | tf_op jit(solution)/shard_map/ppermute | solution.py:513
  86.1 3.9 %collective-permute-done.28.refs_1_ = bf16[640,128]{1,0:T(8,128)(2,1)S(1)} collective-permute-done((bf16[640,128]{1,0:T(8,128)(2,1)S(1)}, bf16[640,128]{1,0:T(8,128)(2,1)S(1)}, u32[]{:S(2)}, u32[]{:S(2)}) %collective-permute-start.28) | collective-permute-done | bytes 163872 | tf_op jit(solution)/shard_map/ppermute | solution.py:513
  (71 shorter events, 15.0 us)
Async XLA Ops:
  0.7 2.3 %copy-start.3 = (bf16[128,1024]{1,0:T(8,128)(2,1)S(1)}, bf16[128,1024]{1,0:T(8,128)(2,1)}, u32[]{:S(2)}) copy-start(bf16[128,1024]{1,0:T(8,128)(2,1)} %refs_2_.5) | copy-start | bytes 786436
  0.7 2.4 %copy-start.4 = (bf16[128,1024]{1,0:T(8,128)(2,1)S(1)}, bf16[128,1024]{1,0:T(8,128)(2,1)}, u32[]{:S(2)}) copy-start(bf16[128,1024]{1,0:T(8,128)(2,1)} %refs_5_.1) | copy-start | bytes 786436
  0.7 2.3 %copy-start.7 = (bf16[1024,128]{1,0:T(8,128)(2,1)S(1)}, bf16[1024,128]{1,0:T(8,128)(2,1)}, u32[]{:S(2)}) copy-start(bf16[1024,128]{1,0:T(8,128)(2,1)} %refs_1_.7) | copy-start | bytes 786436
  4.8 15.0 %collective-permute-start.3 = (bf16[640,256]{1,0:T(8,128)(2,1)S(1)}, bf16[640,256]{1,0:T(8,128)(2,1)S(1)}, u32[]{:S(2)}, u32[]{:S(2)}) collective-permute-start(bf16[640,256]{1,0:T(8,128)(2,1)S(1)} %qd.1.refs_0_), channel_id=1, source_target_pairs={{0,1},{1,0},{2,3},{3,2},{4,5},{5,4},{6,7},{7,6},{8,9},{9,8},{10,11... | collective-permute-start | bytes 983048 | tf_op jit(solution)/shard_map/ppermute | solution.py:412
  4.9 10.2 %collective-permute-start = (bf16[128,256]{1,0:T(8,128)(2,1)S(1)}, bf16[128,256]{1,0:T(8,128)(2,1)S(1)}, u32[]{:S(2)}, u32[]{:S(2)}) collective-permute-start(bf16[128,256]{1,0:T(8,128)(2,1)S(1)} %copy-done.8), channel_id=1, source_target_pairs={{0,0},{1,15},{2,2},{3,1},{4,4},{5,3},{6,6},{7,5},{8,8},{9,7},{10,1... | collective-permute-start | bytes 196616 | tf_op jit(solution)/shard_map/ppermute | solution.py:402
  5.5 9.8 %collective-permute-start.1 = (bf16[128,256]{1,0:T(8,128)(2,1)S(1)}, bf16[128,256]{1,0:T(8,128)(2,1)S(1)}, u32[]{:S(2)}, u32[]{:S(2)}) collective-permute-start(bf16[128,256]{1,0:T(8,128)(2,1)S(1)} %copy-done.8), channel_id=1, source_target_pairs={{0,15},{1,0},{2,1},{3,2},{4,3},{5,4},{6,5},{7,6},{8,7},{9,8},{10,9... | collective-permute-start | bytes 196616 | tf_op jit(solution)/shard_map/ppermute | solution.py:402
  13.5 10.4 %collective-permute-start.4 = (bf16[640,256]{1,0:T(8,128)(2,1)S(1)}, bf16[640,256]{1,0:T(8,128)(2,1)S(1)}, u32[]{:S(2)}, u32[]{:S(2)}) collective-permute-start(bf16[640,256]{1,0:T(8,128)(2,1)S(1)} %qd.1.refs_0_), channel_id=1, source_target_pairs={{0,16},{1,17},{2,18},{3,19},{4,20},{5,21},{6,22},{7,23},{8,24},{9,... | collective-permute-start | bytes 983048 | tf_op jit(solution)/shard_map/ppermute | solution.py:413
  15.4 6.2 %collective-permute-start.2 = (bf16[256,256]{1,0:T(8,128)(2,1)S(1)}, bf16[256,256]{1,0:T(8,128)(2,1)S(1)}, u32[]{:S(2)}, u32[]{:S(2)}) collective-permute-start(bf16[256,256]{1,0:T(8,128)(2,1)S(1)} %constant_dynamic-update-slice_fusion.refs_2_.refs_1_), channel_id=1, source_target_pairs={{0,2},{1,15},{2,4},{3,1},{4,6},{5,3},{6,8},{7,5},{8,10},{9,7},{10,... | collective-permute-start | bytes 393224 | tf_op jit(solution)/shard_map/ppermute | solution.py:403
  16.4 11.0 %collective-permute-start.6 = (bf16[256,256]{1,0:T(8,128)(2,1)S(1)}, bf16[256,256]{1,0:T(8,128)(2,1)S(1)}, u32[]{:S(2)}, u32[]{:S(2)}) collective-permute-start(bf16[256,256]{1,0:T(8,128)(2,1)S(1)} %constant_dynamic-update-slice_fusion.refs_2_.refs_1_), channel_id=1, source_target_pairs={{0,4},{1,13},{2,6},{3,15},{4,8},{5,1},{6,10},{7,3},{8,12},{9,5},{1... | collective-permute-start | bytes 393224 | tf_op jit(solution)/shard_map/ppermute | solution.py:403
  16.4 15.4 %collective-permute-start.7 = (bf16[256,256]{1,0:T(8,128)(2,1)S(1)}, bf16[256,256]{1,0:T(8,128)(2,1)S(1)}, u32[]{:S(2)}, u32[]{:S(2)}) collective-permute-start(bf16[256,256]{1,0:T(8,128)(2,1)S(1)} %constant_dynamic-update-slice_fusion.refs_2_.refs_1_), channel_id=1, source_target_pairs={{0,6},{1,11},{2,8},{3,13},{4,10},{5,15},{6,12},{7,1},{8,14},{9,3},... | collective-permute-start | bytes 393224 | tf_op jit(solution)/shard_map/ppermute | solution.py:403
  23.3 8.5 %collective-permute-start.8 = (bf16[256,384]{1,0:T(8,128)(2,1)S(1)}, bf16[256,384]{1,0:T(8,128)(2,1)S(1)}, u32[]{:S(2)}, u32[]{:S(2)}) collective-permute-start(bf16[256,384]{1,0:T(8,128)(2,1)S(1)} %get-tuple-element.33), channel_id=1, source_target_pairs={{0,64},{32,96},{64,128},{96,160},{128,192},{160,224},{192,0},{224,... | collective-permute-start | bytes 589832 | tf_op jit(solution)/shard_map/ppermute | solution.py:433
  23.8 4.6 %collective-permute-start.5 = (bf16[640,256]{1,0:T(8,128)(2,1)S(1)}, bf16[640,256]{1,0:T(8,128)(2,1)S(1)}, u32[]{:S(2)}, u32[]{:S(2)}) collective-permute-start(bf16[640,256]{1,0:T(8,128)(2,1)S(1)} %collective-permute-done.4.refs_0_), channel_id=1, source_target_pairs={{0,1},{1,0},{2,3},{3,2},{4,5},{5,4},{6,7},{7,6},{8,9},{9,8},{10,11... | collective-permute-start | bytes 983048 | tf_op jit(solution)/shard_map/ppermute | solution.py:414
  33.8 1.4 %collective-permute-start.9 = (f32[16,1280]{1,0:T(8,128)S(1)}, f32[16,1280]{1,0:T(8,128)S(1)}, u32[]{:S(2)}, u32[]{:S(2)}) collective-permute-start(f32[16,1280]{1,0:T(8,128)S(1)} %both_stats.1.refs_0_.refs_4_), channel_id=1, source_target_pairs={{0,1},{1,0},{2,3},{3,2},{4,5},{5,4},{6,7},{7,6},{8,9},{9,8},{10,11... | collective-permute-start | bytes 245768 | tf_op jit(solution)/shard_map/ppermute | solution.py:450
  35.2 4.6 %collective-permute-start.10 = (f32[16,1280]{1,0:T(8,128)S(1)}, f32[16,1280]{1,0:T(8,128)S(1)}, u32[]{:S(2)}, u32[]{:S(2)}) collective-permute-start(f32[16,1280]{1,0:T(8,128)S(1)} %merge.2.refs_0_), channel_id=1, source_target_pairs={{0,16},{1,17},{2,18},{3,19},{4,20},{5,21},{6,22},{7,23},{8,24},{9,... | collective-permute-start | bytes 245768 | tf_op jit(solution)/shard_map/ppermute | solution.py:450
  37.5 12.8 %collective-permute-start.11 = (bf16[256,384]{1,0:T(8,128)(2,1)S(1)}, bf16[256,384]{1,0:T(8,128)(2,1)S(1)}, u32[]{:S(2)}, u32[]{:S(2)}) collective-permute-start(bf16[256,384]{1,0:T(8,128)(2,1)S(1)} %get-tuple-element.38), channel_id=1, source_target_pairs={{0,128},{32,160},{64,192},{96,224},{128,0},{160,32},{192,64},{224,... | collective-permute-start | bytes 589832 | tf_op jit(solution)/shard_map/ppermute | solution.py:443
  39.0 11.3 %collective-permute-start.12 = (bf16[256,384]{1,0:T(8,128)(2,1)S(1)}, bf16[256,384]{1,0:T(8,128)(2,1)S(1)}, u32[]{:S(2)}, u32[]{:S(2)}) collective-permute-start(bf16[256,384]{1,0:T(8,128)(2,1)S(1)} %get-tuple-element.39), channel_id=1, source_target_pairs={{0,192},{32,224},{64,0},{96,32},{128,64},{160,96},{192,128},{224,1... | collective-permute-start | bytes 589832 | tf_op jit(solution)/shard_map/ppermute | solution.py:443
  46.8 11.4 %collective-permute-start.16 = (bf16[256,256]{1,0:T(8,128)(2,1)S(1)}, bf16[256,256]{1,0:T(8,128)(2,1)S(1)}, u32[]{:S(2)}, u32[]{:S(2)}) collective-permute-start(bf16[256,256]{1,0:T(8,128)(2,1)S(1)} %get-tuple-element.37.refs_6_), channel_id=1, source_target_pairs={{6,0},{11,1},{8,2},{13,3},{10,4},{15,5},{12,6},{1,7},{14,8},{3,9},... | collective-permute-start | bytes 393224 | tf_op jit(solution)/shard_map/ppermute | solution.py:458
  47.7 11.4 %collective-permute-start.17 = (bf16[256,256]{1,0:T(8,128)(2,1)S(1)}, bf16[256,256]{1,0:T(8,128)(2,1)S(1)}, u32[]{:S(2)}, u32[]{:S(2)}) collective-permute-start(bf16[256,256]{1,0:T(8,128)(2,1)S(1)} %get-tuple-element.46), channel_id=1, source_target_pairs={{4,0},{13,1},{6,2},{15,3},{8,4},{1,5},{10,6},{3,7},{12,8},{5,9},{1... | collective-permute-start | bytes 393224 | tf_op jit(solution)/shard_map/ppermute | solution.py:458
  54.4 7.2 %collective-permute-start.13 = (bf16[128,640]{1,0:T(8,128)(2,1)S(1)}, bf16[128,640]{1,0:T(8,128)(2,1)S(1)}, u32[]{:S(2)}, u32[]{:S(2)}) collective-permute-start(bf16[128,640]{1,0:T(8,128)(2,1)S(1)} %get-tuple-element.41), channel_id=1, source_target_pairs={{0,16},{1,17},{2,18},{3,19},{4,20},{5,21},{6,22},{7,23},{8,24},{9,... | collective-permute-start | bytes 491528 | tf_op jit(solution)/shard_map/ppermute | solution.py:463
  55.8 6.8 %collective-permute-start.14 = (bf16[128,640]{1,0:T(8,128)(2,1)S(1)}, bf16[128,640]{1,0:T(8,128)(2,1)S(1)}, u32[]{:S(2)}, u32[]{:S(2)}) collective-permute-start(bf16[128,640]{1,0:T(8,128)(2,1)S(1)} %get-tuple-element.42), channel_id=1, source_target_pairs={{0,17},{1,16},{2,19},{3,18},{4,21},{5,20},{6,23},{7,22},{8,25},{9,... | collective-permute-start | bytes 491528 | tf_op jit(solution)/shard_map/ppermute | solution.py:463
  55.8 6.8 %collective-permute-start.15 = (bf16[128,640]{1,0:T(8,128)(2,1)S(1)}, bf16[128,640]{1,0:T(8,128)(2,1)S(1)}, u32[]{:S(2)}, u32[]{:S(2)}) collective-permute-start(bf16[128,640]{1,0:T(8,128)(2,1)S(1)} %get-tuple-element.43), channel_id=1, source_target_pairs={{0,1},{1,0},{2,3},{3,2},{4,5},{5,4},{6,7},{7,6},{8,9},{9,8},{10,11... | collective-permute-start | bytes 491528 | tf_op jit(solution)/shard_map/ppermute | solution.py:463
  58.2 8.0 %collective-permute-start.21 = (bf16[256,256]{1,0:T(8,128)(2,1)S(1)}, bf16[256,256]{1,0:T(8,128)(2,1)S(1)}, u32[]{:S(2)}, u32[]{:S(2)}) collective-permute-start(bf16[256,256]{1,0:T(8,128)(2,1)S(1)} %pair.4.refs_4_), channel_id=1, source_target_pairs={{2,0},{15,1},{4,2},{1,3},{6,4},{3,5},{8,6},{5,7},{10,8},{7,9},{12,... | collective-permute-start | bytes 393224 | tf_op jit(solution)/shard_map/ppermute | solution.py:467
  62.6 8.2 %collective-permute-start.20 = (bf16[128,640]{1,0:T(8,128)(2,1)S(1)}, bf16[128,640]{1,0:T(8,128)(2,1)S(1)}, u32[]{:S(2)}, u32[]{:S(2)}) collective-permute-start(bf16[128,640]{1,0:T(8,128)(2,1)S(1)} %get-tuple-element.47.refs_4_.refs_5_.refs_0_), channel_id=1, source_target_pairs={{0,192},{32,224},{64,0},{96,32},{128,64},{160,96},{192,128},{224,1... | collective-permute-start | bytes 491528 | tf_op jit(solution)/shard_map/ppermute | solution.py:490
  63.2 15.3 %collective-permute-start.18 = (bf16[128,640]{1,0:T(8,128)(2,1)S(1)}, bf16[128,640]{1,0:T(8,128)(2,1)S(1)}, u32[]{:S(2)}, u32[]{:S(2)}) collective-permute-start(bf16[128,640]{1,0:T(8,128)(2,1)S(1)} %get-tuple-element.47.refs_4_.refs_5_.refs_0_), channel_id=1, source_target_pairs={{0,64},{32,96},{64,128},{96,160},{128,192},{160,224},{192,0},{224,... | collective-permute-start | bytes 491528 | tf_op jit(solution)/shard_map/ppermute | solution.py:489
  66.0 11.3 %collective-permute-start.19 = (bf16[128,256]{1,0:T(8,128)(2,1)S(1)}, bf16[128,256]{1,0:T(8,128)(2,1)S(1)}, u32[]{:S(2)}, u32[]{:S(2)}) collective-permute-start(bf16[128,256]{1,0:T(8,128)(2,1)S(1)} %get-tuple-element.48), channel_id=1, source_target_pairs={{0,128},{32,160},{64,192},{96,224},{128,0},{160,32},{192,64},{224,... | collective-permute-start | bytes 196616 | tf_op jit(solution)/shard_map/ppermute | solution.py:491
  66.2 4.8 %collective-permute-start.22 = (bf16[128,256]{1,0:T(8,128)(2,1)S(1)}, bf16[128,256]{1,0:T(8,128)(2,1)S(1)}, u32[]{:S(2)}, u32[]{:S(2)}) collective-permute-start(bf16[128,256]{1,0:T(8,128)(2,1)S(1)} %get-tuple-element.49), channel_id=1, source_target_pairs={{0,0},{15,1},{2,2},{1,3},{4,4},{3,5},{6,6},{5,7},{8,8},{7,9},{10,1... | collective-permute-start | bytes 196616 | tf_op jit(solution)/shard_map/ppermute | solution.py:480
  66.9 7.4 %collective-permute-start.23 = (bf16[128,256]{1,0:T(8,128)(2,1)S(1)}, bf16[128,256]{1,0:T(8,128)(2,1)S(1)}, u32[]{:S(2)}, u32[]{:S(2)}) collective-permute-start(bf16[128,256]{1,0:T(8,128)(2,1)S(1)} %get-tuple-element.50), channel_id=1, source_target_pairs={{15,0},{0,1},{1,2},{2,3},{3,4},{4,5},{5,6},{6,7},{7,8},{8,9},{9,10... | collective-permute-start | bytes 196616 | tf_op jit(solution)/shard_map/ppermute | solution.py:480
  70.9 7.6 %collective-permute-start.27 = (bf16[128,384]{1,0:T(8,128)(2,1)S(1)}, bf16[128,384]{1,0:T(8,128)(2,1)S(1)}, u32[]{:S(2)}, u32[]{:S(2)}) collective-permute-start(bf16[128,384]{1,0:T(8,128)(2,1)S(1)} %slice.4), channel_id=1, source_target_pairs={{0,192},{32,224},{64,0},{96,32},{128,64},{160,96},{192,128},{224,1... | collective-permute-start | bytes 294920 | tf_op jit(solution)/shard_map/ppermute | solution.py:492
  74.3 4.9 %collective-permute-start.24 = (bf16[128,256]{1,0:T(8,128)(2,1)S(1)}, bf16[128,256]{1,0:T(8,128)(2,1)S(1)}, u32[]{:S(2)}, u32[]{:S(2)}) collective-permute-start(bf16[128,256]{1,0:T(8,128)(2,1)S(1)} %piece_sum.1.refs_4_), channel_id=1, source_target_pairs={{0,64},{32,96},{64,128},{96,160},{128,192},{160,224},{192,0},{224,... | collective-permute-start | bytes 196616 | tf_op jit(solution)/shard_map/ppermute | solution.py:379
  75.6 5.9 %collective-permute-start.25 = (bf16[128,256]{1,0:T(8,128)(2,1)S(1)}, bf16[128,256]{1,0:T(8,128)(2,1)S(1)}, u32[]{:S(2)}, u32[]{:S(2)}) collective-permute-start(bf16[128,256]{1,0:T(8,128)(2,1)S(1)} %piece_sum.1.refs_4_), channel_id=1, source_target_pairs={{0,128},{32,160},{64,192},{96,224},{128,0},{160,32},{192,64},{224,... | collective-permute-start | bytes 196616 | tf_op jit(solution)/shard_map/ppermute | solution.py:379
  77.3 5.5 %collective-permute-start.26 = (bf16[128,256]{1,0:T(8,128)(2,1)S(1)}, bf16[128,256]{1,0:T(8,128)(2,1)S(1)}, u32[]{:S(2)}, u32[]{:S(2)}) collective-permute-start(bf16[128,256]{1,0:T(8,128)(2,1)S(1)} %piece_sum.1.refs_4_), channel_id=1, source_target_pairs={{0,192},{32,224},{64,0},{96,32},{128,64},{160,96},{192,128},{224,1... | collective-permute-start | bytes 196616 | tf_op jit(solution)/shard_map/ppermute | solution.py:379
  83.2 6.9 %collective-permute-start.28 = (bf16[640,128]{1,0:T(8,128)(2,1)S(1)}, bf16[640,128]{1,0:T(8,128)(2,1)S(1)}, u32[]{:S(2)}, u32[]{:S(2)}) collective-permute-start(bf16[640,128]{1,0:T(8,128)(2,1)S(1)} %get-tuple-element.55), channel_id=1, source_target_pairs={{0,32},{32,0},{64,96},{96,64},{128,160},{160,128},{192,224},{224,1... | collective-permute-start | bytes 491528 | tf_op jit(solution)/shard_map/ppermute | solution.py:513
  (6 other events, 10.0 us)

commit v3 on v2

--- a/solution.py
+++ b/solution.py
@@ -466,26 +466,26 @@
     (dkv_1,) = pair(weights, rhs, 0, [sds((n, 256), BF16)])
     sums.append(lax.ppermute(dkv_1, TOK, BACK[1]))
     (dkv,) = pair(weights, rhs, n, [sds((n, 256), F32)], after=[dkv_1, *sums[:2]])
+    (x_weights,) = call(
+        stack_kernel,
+        [sds((256, X * 384), BF16)],
+        [place, *x_weights],
+        "stack",
+        smem=1,
+        after=[dkv],
+    )
     cut = 2 * 128
     dq, dq_first = call(
         dq_sum_kernel,
         [sds((128, rows), BF16), sds((128, cut), BF16)],
         [dq_mine, *dq_others],
         "dq_sum",
-        after=[dkv],
+        after=[dkv, x_weights],
     )
     pieces = call(
         pair_sum_kernel, [sds((na, 256), BF16)] * len(RETURN), [dkv, *sums], "pair_sum", after=[dq]
     )
     pieces = [lax.ppermute(piece, TOK, perm) for piece, perm in zip(pieces, RETURN)]
-    (x_weights,) = call(
-        stack_kernel,
-        [sds((256, X * 384), BF16)],
-        [place, *x_weights],
-        "stack",
-        smem=1,
-        after=[dq],
-    )
     back_1 = lax.ppermute(dq, HEAD, SHIFT_X[1])
     back_3 = lax.ppermute(dq, HEAD, SHIFT_X[3])
     back_2a = lax.ppermute(dq_first, HEAD, SHIFT_X[2])

time: 90.9 us -> 89.4 us (0.983)
  waiting for transfers between devices: 20.7 us -> 17.6 us
  starting transfers between devices: 38.7 us -> 39.9 us
    ppermute x2, waiting for transfers between devices: 3.33 us -> 0.51 us  [per_device(): lax.ppermute(piece, TOK, perm)]
    ppermute x1, waiting for transfers between devices: 0.01 us -> 0.91 us  [per_device(): back_2b = lax.ppermute(back_3[:, cut:], HEAD, SHIFT_X[3])]
where the time goes in v3:
time: 89.4 us; the launch traced here: 88.8 us
  starting transfers between devices  39.9 us (45%)
  Pallas kernels  29.4 us (33%)
  waiting for transfers between devices  17.6 us (20%)
  between operations  0.97 us (1%)
    pallas_call x23, Pallas kernels, call(): pl.pallas_call(kernel, out_shape=tuple(outs), in_specs=[spec(i) for i in...  29.4 us
    ppermute x2, starting transfers between devices, per_device(): lax.ppermute(kv, TOK, perm)  8.59 us
    ppermute x3, starting transfers between devices, over_x(): lax.ppermute(array, HEAD, SHIFT_X[r])  4.75 us
    ppermute x3, starting transfers between devices, per_device(): lax.ppermute(block, TOK, FORTH[j])  4.38 us
    ppermute x3, waiting for transfers between devices, per_device(): lax.ppermute(block, TOK, FORTH[j])  4.14 us
    ppermute x1, waiting for transfers between devices, per_device(): lax.ppermute(theirs, HEAD, SWAP_YH)  3.89 us
    ppermute x3, waiting for transfers between devices, over_x(): lax.ppermute(array, HEAD, SHIFT_X[r])  3.4 us
    ppermute x1, starting transfers between devices, per_device(): lax.ppermute(theirs, HEAD, SWAP_YH)  3.02 us
  transfers between devices with their start and end apart: 29, of which 13 were waited for; matrix products, arithmetic and copies ran while one was open for 0% of the time, Pallas kernels for 26%

profile of v3, /device:TPU:6, one launch (start us, length us, event | category | flops | bytes accessed | tf_op | source)
XLA Modules:
  0.0 88.8 jit_solution(16329649997441823047)
XLA Ops:
  0.7 2.3 %kv.1.refs_7_ = bf16[128,256]{1,0:T(8,128)(2,1)} custom-call(bf16[128,1024]{1,0:T(8,128)(2,1)} %refs_0_.3, bf16[1024,128]{1,0:T(8,128)(2,1)} %refs_2_.7, bf16[1024,128]{1,0:T(8,128)(2,1)} %refs_3_.5), custom_call_target="tpu_custom_call" | custom-call | flops 10000000000 | bytes 1000000 | tf_op jit(solution)/shard_map/kv/pallas_call | solution.py:77
  5.5 7.9 %collective-permute-start.1 = (bf16[128,256]{1,0:T(8,128)(2,1)S(1)}, bf16[128,256]{1,0:T(8,128)(2,1)S(1)}, u32[]{:S(2)}, u32[]{:S(2)}) collective-permute-start(bf16[128,256]{1,0:T(8,128)(2,1)S(1)} %copy-done.8), channel_id=1, source_target_pairs={{0,15},{1,0},{2,1},{3,2},{4,3},{5,4},{6,5},{7,6},{8,7},{9,8},{10,9... | collective-permute-start | bytes 196616 | tf_op jit(solution)/shard_map/ppermute | solution.py:402
  13.5 1.6 %collective-permute-start.4 = (bf16[640,256]{1,0:T(8,128)(2,1)S(1)}, bf16[640,256]{1,0:T(8,128)(2,1)S(1)}, u32[]{:S(2)}, u32[]{:S(2)}) collective-permute-start(bf16[640,256]{1,0:T(8,128)(2,1)S(1)} %qd.1.refs_0_), channel_id=1, source_target_pairs={{0,16},{1,17},{2,18},{3,19},{4,20},{5,21},{6,22},{7,23},{8,24},{9,... | collective-permute-start | bytes 983048 | tf_op jit(solution)/shard_map/ppermute | solution.py:413
  15.4 1.0 %collective-permute-start.2 = (bf16[256,256]{1,0:T(8,128)(2,1)S(1)}, bf16[256,256]{1,0:T(8,128)(2,1)S(1)}, u32[]{:S(2)}, u32[]{:S(2)}) collective-permute-start(bf16[256,256]{1,0:T(8,128)(2,1)S(1)} %constant_dynamic-update-slice_fusion.refs_2_.refs_1_), channel_id=1, source_target_pairs={{0,2},{1,15},{2,4},{3,1},{4,6},{5,3},{6,8},{7,5},{8,10},{9,7},{10,... | collective-permute-start | bytes 393224 | tf_op jit(solution)/shard_map/ppermute | solution.py:403
  16.4 3.4 %collective-permute-start.7 = (bf16[256,256]{1,0:T(8,128)(2,1)S(1)}, bf16[256,256]{1,0:T(8,128)(2,1)S(1)}, u32[]{:S(2)}, u32[]{:S(2)}) collective-permute-start(bf16[256,256]{1,0:T(8,128)(2,1)S(1)} %constant_dynamic-update-slice_fusion.refs_2_.refs_1_), channel_id=1, source_target_pairs={{0,6},{1,11},{2,8},{3,13},{4,10},{5,15},{6,12},{7,1},{8,14},{9,3},... | collective-permute-start | bytes 393224 | tf_op jit(solution)/shard_map/ppermute | solution.py:403
  19.8 1.2 %first_stats.2 = (f32[8,1280]{1,0:T(8,128)S(1)}, bf16[2560,256]{1,0:T(8,128)(2,1)S(1)}) custom-call(bf16[640,256]{1,0:T(8,128)(2,1)S(1)} %qd.1.refs_0_, bf16[640,256]{1,0:T(8,128)(2,1)S(1)} %collective-permute-done.3.refs_1_, bf16[256,256]{1,0:T(8,128)(2,1)S(1)} %constant_dynamic-update-slice_fusion.refs_2_.refs_1_), custom_call_target="tpu_custom_call" | custom-call | flops 10000000000 | bytes 1000000 | tf_op jit(solution)/shard_map/first_stats/pallas_call | solution.py:77
  21.6 1.1 %stats.2.refs_2_.refs_4_ = f32[8,1280]{1,0:T(8,128)S(1)} custom-call(bf16[256,256]{1,0:T(8,128)(2,1)S(1)} %collective-permute-done.2.refs_3_.refs_0_, bf16[2560,256]{1,0:T(8,128)(2,1)S(1)} %get-tuple-element.29.refs_1_.refs_2_, f32[8,1280]{1,0:T(8,128)S(1)} %get-tuple-element.31.refs_2_), custom_call_target="tpu_custom_call" | custom-call | flops 10000000000 | bytes 1000000 | tf_op jit(solution)/shard_map/stats/pallas_call | solution.py:77
  23.8 3.6 %collective-permute-done.6.refs_4_.refs_0_.refs_1_ = bf16[256,256]{1,0:T(8,128)(2,1)S(1)} collective-permute-done((bf16[256,256]{1,0:T(8,128)(2,1)S(1)}, bf16[256,256]{1,0:T(8,128)(2,1)S(1)}, u32[]{:S(2)}, u32[]{:S(2)}) %collective-permute-start.6) | collective-permute-done | bytes 131104 | tf_op jit(solution)/shard_map/ppermute | solution.py:403
  27.4 1.1 %stats.3.refs_3_ = f32[8,1280]{1,0:T(8,128)S(1)} custom-call(bf16[256,256]{1,0:T(8,128)(2,1)S(1)} %collective-permute-done.6.refs_4_.refs_0_.refs_1_, bf16[2560,256]{1,0:T(8,128)(2,1)S(1)} %get-tuple-element.29.refs_1_.refs_2_, f32[8,1280]{1,0:T(8,128)S(1)} %stats.2.refs_2_.refs_4_), custom_call_target="tpu_custom_call" | custom-call | flops 10000000000 | bytes 1000000 | tf_op jit(solution)/shard_map/stats/pallas_call | solution.py:77
  28.5 3.3 %first_stats.3 = (f32[8,1280]{1,0:T(8,128)S(1)}, bf16[2560,256]{1,0:T(8,128)(2,1)S(1)}) custom-call(bf16[640,256]{1,0:T(8,128)(2,1)S(1)} %collective-permute-done.4.refs_0_, bf16[640,256]{1,0:T(8,128)(2,1)S(1)} %collective-permute-done.5.refs_1_, bf16[256,256]{1,0:T(8,128)(2,1)S(1)} %constant_dynamic-update-slice_fusion.refs_2_.refs_1_, ...), custom_call_target="tpu_custom_call" | custom-call | flops 10000000000 | bytes 1000000 | tf_op jit(solution)/shard_map/first_stats/pallas_call | solution.py:77
  31.8 1.9 %both_stats.1.refs_0_.refs_4_ = f32[16,1280]{1,0:T(8,128)S(1)} custom-call(bf16[256,256]{1,0:T(8,128)(2,1)S(1)} %collective-permute-done.7.refs_0_, bf16[2560,256]{1,0:T(8,128)(2,1)S(1)} %get-tuple-element.29.refs_1_.refs_2_, bf16[2560,256]{1,0:T(8,128)(2,1)S(1)} %get-tuple-element.30.refs_2_.refs_3_, f32[8,1280]{1,0:T(8,128)S(1)} %stats.3.refs_3_, ...), custom_call_target="tpu_custom_call" | custom-call | flops 10000000000 | bytes 1000000 | tf_op jit(solution)/shard_map/both_stats/pallas_call | solution.py:77
  33.8 1.3 %collective-permute-done.9.refs_1_ = f32[16,1280]{1,0:T(8,128)S(1)} collective-permute-done((f32[16,1280]{1,0:T(8,128)S(1)}, f32[16,1280]{1,0:T(8,128)S(1)}, u32[]{:S(2)}, u32[]{:S(2)}) %collective-permute-start.9) | collective-permute-done | bytes 81952 | tf_op jit(solution)/shard_map/ppermute | solution.py:450
  35.1 1.7 %collective-permute-start.10 = (f32[16,1280]{1,0:T(8,128)S(1)}, f32[16,1280]{1,0:T(8,128)S(1)}, u32[]{:S(2)}, u32[]{:S(2)}) collective-permute-start(f32[16,1280]{1,0:T(8,128)S(1)} %merge.2.refs_0_), channel_id=1, source_target_pairs={{0,16},{1,17},{2,18},{3,19},{4,20},{5,21},{6,22},{7,23},{8,24},{9,... | collective-permute-start | bytes 245768 | tf_op jit(solution)/shard_map/ppermute | solution.py:450
  37.4 1.5 %collective-permute-start.11 = (bf16[256,384]{1,0:T(8,128)(2,1)S(1)}, bf16[256,384]{1,0:T(8,128)(2,1)S(1)}, u32[]{:S(2)}, u32[]{:S(2)}) collective-permute-start(bf16[256,384]{1,0:T(8,128)(2,1)S(1)} %get-tuple-element.38), channel_id=1, source_target_pairs={{0,128},{32,160},{64,192},{96,224},{128,0},{160,32},{192,64},{224,... | collective-permute-start | bytes 589832 | tf_op jit(solution)/shard_map/ppermute | solution.py:443
  39.8 4.1 %scores.2 = (bf16[512,5120]{1,0:T(8,128)(2,1)S(1)}, bf16[512,5120]{1,0:T(8,128)(2,1)S(1)}, f32[128,2560]{1,0:T(8,128)S(1)}) custom-call(bf16[256,256]{1,0:T(8,128)(2,1)S(1)} %collective-permute-done.7.refs_0_, bf16[256,256]{1,0:T(8,128)(2,1)S(1)} %collective-permute-done.6.refs_4_.refs_0_.refs_1_, bf16[2560,256]{1,0:T(8,128)(2,1)S(1)} %get-tuple-element.29.refs_1_.refs_2_, ...), custom_call_target="tpu_custom_call" | custom-call | flops 1500000000 | bytes 1000000 | tf_op jit(solution)/shard_map/scores/pallas_call | solution.py:77
  43.9 2.9 %pair.3 = (bf16[256,256]{1,0:T(8,128)(2,1)S(1)}, bf16[256,256]{1,0:T(8,128)(2,1)S(1)}) custom-call(bf16[512,5120]{1,0:T(8,128)(2,1)S(1)} %get-tuple-element.35.refs_0_, bf16[512,5120]{1,0:T(8,128)(2,1)S(1)} %get-tuple-element.36.refs_1_, bf16[2560,256]{1,0:T(8,128)(2,1)S(1)} %get-tuple-element.29.refs_1_.refs_2_, ...), custom_call_target="tpu_custom_call" | custom-call | flops 1500000000 | bytes 1000000 | tf_op jit(solution)/shard_map/pair/pallas_call | solution.py:77
  47.6 2.6 %collective-permute-start.17 = (bf16[256,256]{1,0:T(8,128)(2,1)S(1)}, bf16[256,256]{1,0:T(8,128)(2,1)S(1)}, u32[]{:S(2)}, u32[]{:S(2)}) collective-permute-start(bf16[256,256]{1,0:T(8,128)(2,1)S(1)} %get-tuple-element.46), channel_id=1, source_target_pairs={{4,0},{13,1},{6,2},{15,3},{8,4},{1,5},{10,6},{3,7},{12,8},{5,9},{1... | collective-permute-start | bytes 393224 | tf_op jit(solution)/shard_map/ppermute | solution.py:458
  50.2 4.2 %scores.3 = (bf16[512,5120]{1,0:T(8,128)(2,1)S(1)}, bf16[512,5120]{1,0:T(8,128)(2,1)S(1)}, f32[128,640]{1,0:T(8,128)S(1)}, bf16[128,640]{1,0:T(8,128)(2,1)S(1)},...) custom-call(bf16[256,256]{1,0:T(8,128)(2,1)S(1)} %collective-permute-done.2.refs_3_.refs_0_, ...), custom_call_target="tpu_custom_call" | custom-call | flops 1500000000 | bytes 1000000 | tf_op jit(solution)/shard_map/scores/pallas_call | solution.py:77
  54.4 1.3 %collective-permute-start.13 = (bf16[128,640]{1,0:T(8,128)(2,1)S(1)}, bf16[128,640]{1,0:T(8,128)(2,1)S(1)}, u32[]{:S(2)}, u32[]{:S(2)}) collective-permute-start(bf16[128,640]{1,0:T(8,128)(2,1)S(1)} %get-tuple-element.41), channel_id=1, source_target_pairs={{0,16},{1,17},{2,18},{3,19},{4,20},{5,21},{6,22},{7,23},{8,24},{9,... | collective-permute-start | bytes 491528 | tf_op jit(solution)/shard_map/ppermute | solution.py:463
  55.8 0.9 %collective-permute-start.15 = (bf16[128,640]{1,0:T(8,128)(2,1)S(1)}, bf16[128,640]{1,0:T(8,128)(2,1)S(1)}, u32[]{:S(2)}, u32[]{:S(2)}) collective-permute-start(bf16[128,640]{1,0:T(8,128)(2,1)S(1)} %get-tuple-element.43), channel_id=1, source_target_pairs={{0,1},{1,0},{2,3},{3,2},{4,5},{5,4},{6,7},{7,6},{8,9},{9,8},{10,11... | collective-permute-start | bytes 491528 | tf_op jit(solution)/shard_map/ppermute | solution.py:463
  56.6 1.5 %pair.4.refs_4_ = bf16[256,256]{1,0:T(8,128)(2,1)S(1)} custom-call(bf16[512,5120]{1,0:T(8,128)(2,1)S(1)} %get-tuple-element.44.refs_0_, bf16[512,5120]{1,0:T(8,128)(2,1)S(1)} %get-tuple-element.45.refs_1_, bf16[2560,256]{1,0:T(8,128)(2,1)S(1)} %get-tuple-element.29.refs_1_.refs_2_, bf16[2560,256]{1,0:T(8,128)(2,1)S(1)} %get-tuple-element.30.refs_2_.refs_3_), custom_call_target="tpu_custom_call" | custom-call | flops 1500000000 | bytes 1000000 | tf_op jit(solution)/shard_map/pair/pallas_call | solution.py:77
  59.0 1.5 %pair.5.refs_5_.refs_4_.refs_0_ = f32[256,256]{1,0:T(8,128)S(1)} custom-call(bf16[512,5120]{1,0:T(8,128)(2,1)S(1)} %get-tuple-element.44.refs_0_, bf16[512,5120]{1,0:T(8,128)(2,1)S(1)} %get-tuple-element.45.refs_1_, bf16[2560,256]{1,0:T(8,128)(2,1)S(1)} %get-tuple-element.29.refs_1_.refs_2_, bf16[2560,256]{1,0:T(8,128)(2,1)S(1)} %get-tuple-element.30.refs_2_.refs_3_, ...), custom_call_target="tpu_custom_call" | custom-call | flops 1500000000 | bytes 1000000 | tf_op jit(solution)/shard_map/pair/pallas_call | solution.py:77
  64.0 2.2 %collective-permute-start.23 = (bf16[128,256]{1,0:T(8,128)(2,1)S(1)}, bf16[128,256]{1,0:T(8,128)(2,1)S(1)}, u32[]{:S(2)}, u32[]{:S(2)}) collective-permute-start(bf16[128,256]{1,0:T(8,128)(2,1)S(1)} %get-tuple-element.51), channel_id=1, source_target_pairs={{15,0},{0,1},{1,2},{2,3},{3,4},{4,5},{5,6},{6,7},{7,8},{8,9},{9,10... | collective-permute-start | bytes 196616 | tf_op jit(solution)/shard_map/ppermute | solution.py:488
  66.2 2.6 %collective-permute-start.18 = (bf16[128,640]{1,0:T(8,128)(2,1)S(1)}, bf16[128,640]{1,0:T(8,128)(2,1)S(1)}, u32[]{:S(2)}, u32[]{:S(2)}) collective-permute-start(bf16[128,640]{1,0:T(8,128)(2,1)S(1)} %get-tuple-element.48.refs_4_.refs_0_), channel_id=1, source_target_pairs={{0,64},{32,96},{64,128},{96,160},{128,192},{160,224},{192,0},{224,... | collective-permute-start | bytes 491528 | tf_op jit(solution)/shard_map/ppermute | solution.py:489
  68.8 0.9 %collective-permute-start.19 = (bf16[128,256]{1,0:T(8,128)(2,1)S(1)}, bf16[128,256]{1,0:T(8,128)(2,1)S(1)}, u32[]{:S(2)}, u32[]{:S(2)}) collective-permute-start(bf16[128,256]{1,0:T(8,128)(2,1)S(1)} %get-tuple-element.49), channel_id=1, source_target_pairs={{0,128},{32,160},{64,192},{96,224},{128,0},{160,32},{192,64},{224,... | collective-permute-start | bytes 196616 | tf_op jit(solution)/shard_map/ppermute | solution.py:491
  69.7 1.0 %collective-permute-done.20.refs_4_.refs_3_ = bf16[128,640]{1,0:T(8,128)(2,1)S(1)} collective-permute-done((bf16[128,640]{1,0:T(8,128)(2,1)S(1)}, bf16[128,640]{1,0:T(8,128)(2,1)S(1)}, u32[]{:S(2)}, u32[]{:S(2)}) %collective-permute-start.20) | collective-permute-done | bytes 163872 | tf_op jit(solution)/shard_map/ppermute | solution.py:490
  71.4 2.8 %collective-permute-start.24 = (bf16[128,256]{1,0:T(8,128)(2,1)S(1)}, bf16[128,256]{1,0:T(8,128)(2,1)S(1)}, u32[]{:S(2)}, u32[]{:S(2)}) collective-permute-start(bf16[128,256]{1,0:T(8,128)(2,1)S(1)} %piece_sum.1.refs_4_), channel_id=1, source_target_pairs={{0,64},{32,96},{64,128},{96,160},{128,192},{160,224},{192,0},{224,... | collective-permute-start | bytes 196616 | tf_op jit(solution)/shard_map/ppermute | solution.py:379
  75.0 1.2 %collective-permute-start.26 = (bf16[128,256]{1,0:T(8,128)(2,1)S(1)}, bf16[128,256]{1,0:T(8,128)(2,1)S(1)}, u32[]{:S(2)}, u32[]{:S(2)}) collective-permute-start(bf16[128,256]{1,0:T(8,128)(2,1)S(1)} %piece_sum.1.refs_4_), channel_id=1, source_target_pairs={{0,192},{32,224},{64,0},{96,32},{128,64},{160,96},{192,128},{224,1... | collective-permute-start | bytes 196616 | tf_op jit(solution)/shard_map/ppermute | solution.py:379
  76.1 0.9 %collective-permute-done.27.refs_3_ = bf16[128,384]{1,0:T(8,128)(2,1)S(1)} collective-permute-done((bf16[128,384]{1,0:T(8,128)(2,1)S(1)}, bf16[128,384]{1,0:T(8,128)(2,1)S(1)}, u32[]{:S(2)}, u32[]{:S(2)}) %collective-permute-start.27) | collective-permute-done | bytes 98336 | tf_op jit(solution)/shard_map/ppermute | solution.py:492
  77.4 2.7 %collective-permute-done.25.refs_6_ = bf16[128,256]{1,0:T(8,128)(2,1)S(1)} collective-permute-done((bf16[128,256]{1,0:T(8,128)(2,1)S(1)}, bf16[128,256]{1,0:T(8,128)(2,1)S(1)}, u32[]{:S(2)}, u32[]{:S(2)}) %collective-permute-start.25) | collective-permute-done | bytes 65568 | tf_op jit(solution)/shard_map/ppermute | solution.py:379
  81.2 3.0 %collective-permute-start.28 = (bf16[640,128]{1,0:T(8,128)(2,1)S(1)}, bf16[640,128]{1,0:T(8,128)(2,1)S(1)}, u32[]{:S(2)}, u32[]{:S(2)}) collective-permute-start(bf16[640,128]{1,0:T(8,128)(2,1)S(1)} %get-tuple-element.55), channel_id=1, source_target_pairs={{0,32},{32,0},{64,96},{96,64},{128,160},{160,128},{192,224},{224,1... | collective-permute-start | bytes 491528 | tf_op jit(solution)/shard_map/ppermute | solution.py:513
  84.2 3.9 %collective-permute-done.28.refs_1_ = bf16[640,128]{1,0:T(8,128)(2,1)S(1)} collective-permute-done((bf16[640,128]{1,0:T(8,128)(2,1)S(1)}, bf16[640,128]{1,0:T(8,128)(2,1)S(1)}, u32[]{:S(2)}, u32[]{:S(2)}) %collective-permute-start.28) | collective-permute-done | bytes 163872 | tf_op jit(solution)/shard_map/ppermute | solution.py:513
  (71 shorter events, 14.8 us)
Async XLA Ops:
  0.7 2.3 %copy-start.3 = (bf16[128,1024]{1,0:T(8,128)(2,1)S(1)}, bf16[128,1024]{1,0:T(8,128)(2,1)}, u32[]{:S(2)}) copy-start(bf16[128,1024]{1,0:T(8,128)(2,1)} %refs_2_.5) | copy-start | bytes 786436
  0.7 2.4 %copy-start.4 = (bf16[128,1024]{1,0:T(8,128)(2,1)S(1)}, bf16[128,1024]{1,0:T(8,128)(2,1)}, u32[]{:S(2)}) copy-start(bf16[128,1024]{1,0:T(8,128)(2,1)} %refs_5_.1) | copy-start | bytes 786436
  0.7 2.3 %copy-start.7 = (bf16[1024,128]{1,0:T(8,128)(2,1)S(1)}, bf16[1024,128]{1,0:T(8,128)(2,1)}, u32[]{:S(2)}) copy-start(bf16[1024,128]{1,0:T(8,128)(2,1)} %refs_1_.7) | copy-start | bytes 786436
  4.8 15.0 %collective-permute-start.3 = (bf16[640,256]{1,0:T(8,128)(2,1)S(1)}, bf16[640,256]{1,0:T(8,128)(2,1)S(1)}, u32[]{:S(2)}, u32[]{:S(2)}) collective-permute-start(bf16[640,256]{1,0:T(8,128)(2,1)S(1)} %qd.1.refs_0_), channel_id=1, source_target_pairs={{0,1},{1,0},{2,3},{3,2},{4,5},{5,4},{6,7},{7,6},{8,9},{9,8},{10,11... | collective-permute-start | bytes 983048 | tf_op jit(solution)/shard_map/ppermute | solution.py:412
  4.9 10.2 %collective-permute-start = (bf16[128,256]{1,0:T(8,128)(2,1)S(1)}, bf16[128,256]{1,0:T(8,128)(2,1)S(1)}, u32[]{:S(2)}, u32[]{:S(2)}) collective-permute-start(bf16[128,256]{1,0:T(8,128)(2,1)S(1)} %copy-done.8), channel_id=1, source_target_pairs={{0,0},{1,15},{2,2},{3,1},{4,4},{5,3},{6,6},{7,5},{8,8},{9,7},{10,1... | collective-permute-start | bytes 196616 | tf_op jit(solution)/shard_map/ppermute | solution.py:402
  5.5 9.8 %collective-permute-start.1 = (bf16[128,256]{1,0:T(8,128)(2,1)S(1)}, bf16[128,256]{1,0:T(8,128)(2,1)S(1)}, u32[]{:S(2)}, u32[]{:S(2)}) collective-permute-start(bf16[128,256]{1,0:T(8,128)(2,1)S(1)} %copy-done.8), channel_id=1, source_target_pairs={{0,15},{1,0},{2,1},{3,2},{4,3},{5,4},{6,5},{7,6},{8,7},{9,8},{10,9... | collective-permute-start | bytes 196616 | tf_op jit(solution)/shard_map/ppermute | solution.py:402
  13.5 10.4 %collective-permute-start.4 = (bf16[640,256]{1,0:T(8,128)(2,1)S(1)}, bf16[640,256]{1,0:T(8,128)(2,1)S(1)}, u32[]{:S(2)}, u32[]{:S(2)}) collective-permute-start(bf16[640,256]{1,0:T(8,128)(2,1)S(1)} %qd.1.refs_0_), channel_id=1, source_target_pairs={{0,16},{1,17},{2,18},{3,19},{4,20},{5,21},{6,22},{7,23},{8,24},{9,... | collective-permute-start | bytes 983048 | tf_op jit(solution)/shard_map/ppermute | solution.py:413
  15.4 6.2 %collective-permute-start.2 = (bf16[256,256]{1,0:T(8,128)(2,1)S(1)}, bf16[256,256]{1,0:T(8,128)(2,1)S(1)}, u32[]{:S(2)}, u32[]{:S(2)}) collective-permute-start(bf16[256,256]{1,0:T(8,128)(2,1)S(1)} %constant_dynamic-update-slice_fusion.refs_2_.refs_1_), channel_id=1, source_target_pairs={{0,2},{1,15},{2,4},{3,1},{4,6},{5,3},{6,8},{7,5},{8,10},{9,7},{10,... | collective-permute-start | bytes 393224 | tf_op jit(solution)/shard_map/ppermute | solution.py:403
  16.4 11.0 %collective-permute-start.6 = (bf16[256,256]{1,0:T(8,128)(2,1)S(1)}, bf16[256,256]{1,0:T(8,128)(2,1)S(1)}, u32[]{:S(2)}, u32[]{:S(2)}) collective-permute-start(bf16[256,256]{1,0:T(8,128)(2,1)S(1)} %constant_dynamic-update-slice_fusion.refs_2_.refs_1_), channel_id=1, source_target_pairs={{0,4},{1,13},{2,6},{3,15},{4,8},{5,1},{6,10},{7,3},{8,12},{9,5},{1... | collective-permute-start | bytes 393224 | tf_op jit(solution)/shard_map/ppermute | solution.py:403
  16.4 15.4 %collective-permute-start.7 = (bf16[256,256]{1,0:T(8,128)(2,1)S(1)}, bf16[256,256]{1,0:T(8,128)(2,1)S(1)}, u32[]{:S(2)}, u32[]{:S(2)}) collective-permute-start(bf16[256,256]{1,0:T(8,128)(2,1)S(1)} %constant_dynamic-update-slice_fusion.refs_2_.refs_1_), channel_id=1, source_target_pairs={{0,6},{1,11},{2,8},{3,13},{4,10},{5,15},{6,12},{7,1},{8,14},{9,3},... | collective-permute-start | bytes 393224 | tf_op jit(solution)/shard_map/ppermute | solution.py:403
  23.3 8.5 %collective-permute-start.8 = (bf16[256,384]{1,0:T(8,128)(2,1)S(1)}, bf16[256,384]{1,0:T(8,128)(2,1)S(1)}, u32[]{:S(2)}, u32[]{:S(2)}) collective-permute-start(bf16[256,384]{1,0:T(8,128)(2,1)S(1)} %get-tuple-element.33), channel_id=1, source_target_pairs={{0,64},{32,96},{64,128},{96,160},{128,192},{160,224},{192,0},{224,... | collective-permute-start | bytes 589832 | tf_op jit(solution)/shard_map/ppermute | solution.py:433
  23.8 4.6 %collective-permute-start.5 = (bf16[640,256]{1,0:T(8,128)(2,1)S(1)}, bf16[640,256]{1,0:T(8,128)(2,1)S(1)}, u32[]{:S(2)}, u32[]{:S(2)}) collective-permute-start(bf16[640,256]{1,0:T(8,128)(2,1)S(1)} %collective-permute-done.4.refs_0_), channel_id=1, source_target_pairs={{0,1},{1,0},{2,3},{3,2},{4,5},{5,4},{6,7},{7,6},{8,9},{9,8},{10,11... | collective-permute-start | bytes 983048 | tf_op jit(solution)/shard_map/ppermute | solution.py:414
  33.7 1.4 %collective-permute-start.9 = (f32[16,1280]{1,0:T(8,128)S(1)}, f32[16,1280]{1,0:T(8,128)S(1)}, u32[]{:S(2)}, u32[]{:S(2)}) collective-permute-start(f32[16,1280]{1,0:T(8,128)S(1)} %both_stats.1.refs_0_.refs_4_), channel_id=1, source_target_pairs={{0,1},{1,0},{2,3},{3,2},{4,5},{5,4},{6,7},{7,6},{8,9},{9,8},{10,11... | collective-permute-start | bytes 245768 | tf_op jit(solution)/shard_map/ppermute | solution.py:450
  35.1 4.6 %collective-permute-start.10 = (f32[16,1280]{1,0:T(8,128)S(1)}, f32[16,1280]{1,0:T(8,128)S(1)}, u32[]{:S(2)}, u32[]{:S(2)}) collective-permute-start(f32[16,1280]{1,0:T(8,128)S(1)} %merge.2.refs_0_), channel_id=1, source_target_pairs={{0,16},{1,17},{2,18},{3,19},{4,20},{5,21},{6,22},{7,23},{8,24},{9,... | collective-permute-start | bytes 245768 | tf_op jit(solution)/shard_map/ppermute | solution.py:450
  37.4 12.8 %collective-permute-start.11 = (bf16[256,384]{1,0:T(8,128)(2,1)S(1)}, bf16[256,384]{1,0:T(8,128)(2,1)S(1)}, u32[]{:S(2)}, u32[]{:S(2)}) collective-permute-start(bf16[256,384]{1,0:T(8,128)(2,1)S(1)} %get-tuple-element.38), channel_id=1, source_target_pairs={{0,128},{32,160},{64,192},{96,224},{128,0},{160,32},{192,64},{224,... | collective-permute-start | bytes 589832 | tf_op jit(solution)/shard_map/ppermute | solution.py:443
  38.9 11.3 %collective-permute-start.12 = (bf16[256,384]{1,0:T(8,128)(2,1)S(1)}, bf16[256,384]{1,0:T(8,128)(2,1)S(1)}, u32[]{:S(2)}, u32[]{:S(2)}) collective-permute-start(bf16[256,384]{1,0:T(8,128)(2,1)S(1)} %get-tuple-element.39), channel_id=1, source_target_pairs={{0,192},{32,224},{64,0},{96,32},{128,64},{160,96},{192,128},{224,1... | collective-permute-start | bytes 589832 | tf_op jit(solution)/shard_map/ppermute | solution.py:443
  46.8 11.4 %collective-permute-start.16 = (bf16[256,256]{1,0:T(8,128)(2,1)S(1)}, bf16[256,256]{1,0:T(8,128)(2,1)S(1)}, u32[]{:S(2)}, u32[]{:S(2)}) collective-permute-start(bf16[256,256]{1,0:T(8,128)(2,1)S(1)} %get-tuple-element.37.refs_6_), channel_id=1, source_target_pairs={{6,0},{11,1},{8,2},{13,3},{10,4},{15,5},{12,6},{1,7},{14,8},{3,9},... | collective-permute-start | bytes 393224 | tf_op jit(solution)/shard_map/ppermute | solution.py:458
  47.6 11.4 %collective-permute-start.17 = (bf16[256,256]{1,0:T(8,128)(2,1)S(1)}, bf16[256,256]{1,0:T(8,128)(2,1)S(1)}, u32[]{:S(2)}, u32[]{:S(2)}) collective-permute-start(bf16[256,256]{1,0:T(8,128)(2,1)S(1)} %get-tuple-element.46), channel_id=1, source_target_pairs={{4,0},{13,1},{6,2},{15,3},{8,4},{1,5},{10,6},{3,7},{12,8},{5,9},{1... | collective-permute-start | bytes 393224 | tf_op jit(solution)/shard_map/ppermute | solution.py:458
  54.4 7.2 %collective-permute-start.13 = (bf16[128,640]{1,0:T(8,128)(2,1)S(1)}, bf16[128,640]{1,0:T(8,128)(2,1)S(1)}, u32[]{:S(2)}, u32[]{:S(2)}) collective-permute-start(bf16[128,640]{1,0:T(8,128)(2,1)S(1)} %get-tuple-element.41), channel_id=1, source_target_pairs={{0,16},{1,17},{2,18},{3,19},{4,20},{5,21},{6,22},{7,23},{8,24},{9,... | collective-permute-start | bytes 491528 | tf_op jit(solution)/shard_map/ppermute | solution.py:463
  55.8 6.7 %collective-permute-start.14 = (bf16[128,640]{1,0:T(8,128)(2,1)S(1)}, bf16[128,640]{1,0:T(8,128)(2,1)S(1)}, u32[]{:S(2)}, u32[]{:S(2)}) collective-permute-start(bf16[128,640]{1,0:T(8,128)(2,1)S(1)} %get-tuple-element.42), channel_id=1, source_target_pairs={{0,17},{1,16},{2,19},{3,18},{4,21},{5,20},{6,23},{7,22},{8,25},{9,... | collective-permute-start | bytes 491528 | tf_op jit(solution)/shard_map/ppermute | solution.py:463
  55.8 6.7 %collective-permute-start.15 = (bf16[128,640]{1,0:T(8,128)(2,1)S(1)}, bf16[128,640]{1,0:T(8,128)(2,1)S(1)}, u32[]{:S(2)}, u32[]{:S(2)}) collective-permute-start(bf16[128,640]{1,0:T(8,128)(2,1)S(1)} %get-tuple-element.43), channel_id=1, source_target_pairs={{0,1},{1,0},{2,3},{3,2},{4,5},{5,4},{6,7},{7,6},{8,9},{9,8},{10,11... | collective-permute-start | bytes 491528 | tf_op jit(solution)/shard_map/ppermute | solution.py:463
  58.2 5.0 %collective-permute-start.21 = (bf16[256,256]{1,0:T(8,128)(2,1)S(1)}, bf16[256,256]{1,0:T(8,128)(2,1)S(1)}, u32[]{:S(2)}, u32[]{:S(2)}) collective-permute-start(bf16[256,256]{1,0:T(8,128)(2,1)S(1)} %pair.4.refs_4_), channel_id=1, source_target_pairs={{2,0},{15,1},{4,2},{1,3},{6,4},{3,5},{8,6},{5,7},{10,8},{7,9},{12,... | collective-permute-start | bytes 393224 | tf_op jit(solution)/shard_map/ppermute | solution.py:467
  62.6 8.2 %collective-permute-start.20 = (bf16[128,640]{1,0:T(8,128)(2,1)S(1)}, bf16[128,640]{1,0:T(8,128)(2,1)S(1)}, u32[]{:S(2)}, u32[]{:S(2)}) collective-permute-start(bf16[128,640]{1,0:T(8,128)(2,1)S(1)} %get-tuple-element.48.refs_4_.refs_0_), channel_id=1, source_target_pairs={{0,192},{32,224},{64,0},{96,32},{128,64},{160,96},{192,128},{224,1... | collective-permute-start | bytes 491528 | tf_op jit(solution)/shard_map/ppermute | solution.py:490
  63.3 7.5 %collective-permute-start.22 = (bf16[128,256]{1,0:T(8,128)(2,1)S(1)}, bf16[128,256]{1,0:T(8,128)(2,1)S(1)}, u32[]{:S(2)}, u32[]{:S(2)}) collective-permute-start(bf16[128,256]{1,0:T(8,128)(2,1)S(1)} %get-tuple-element.50), channel_id=1, source_target_pairs={{0,0},{15,1},{2,2},{1,3},{4,4},{3,5},{6,6},{5,7},{8,8},{7,9},{10,1... | collective-permute-start | bytes 196616 | tf_op jit(solution)/shard_map/ppermute | solution.py:488
  64.0 7.4 %collective-permute-start.23 = (bf16[128,256]{1,0:T(8,128)(2,1)S(1)}, bf16[128,256]{1,0:T(8,128)(2,1)S(1)}, u32[]{:S(2)}, u32[]{:S(2)}) collective-permute-start(bf16[128,256]{1,0:T(8,128)(2,1)S(1)} %get-tuple-element.51), channel_id=1, source_target_pairs={{15,0},{0,1},{1,2},{2,3},{3,4},{4,5},{5,6},{6,7},{7,8},{8,9},{9,10... | collective-permute-start | bytes 196616 | tf_op jit(solution)/shard_map/ppermute | solution.py:488
  66.2 9.9 %collective-permute-start.18 = (bf16[128,640]{1,0:T(8,128)(2,1)S(1)}, bf16[128,640]{1,0:T(8,128)(2,1)S(1)}, u32[]{:S(2)}, u32[]{:S(2)}) collective-permute-start(bf16[128,640]{1,0:T(8,128)(2,1)S(1)} %get-tuple-element.48.refs_4_.refs_0_), channel_id=1, source_target_pairs={{0,64},{32,96},{64,128},{96,160},{128,192},{160,224},{192,0},{224,... | collective-permute-start | bytes 491528 | tf_op jit(solution)/shard_map/ppermute | solution.py:489
  68.8 6.2 %collective-permute-start.19 = (bf16[128,256]{1,0:T(8,128)(2,1)S(1)}, bf16[128,256]{1,0:T(8,128)(2,1)S(1)}, u32[]{:S(2)}, u32[]{:S(2)}) collective-permute-start(bf16[128,256]{1,0:T(8,128)(2,1)S(1)} %get-tuple-element.49), channel_id=1, source_target_pairs={{0,128},{32,160},{64,192},{96,224},{128,0},{160,32},{192,64},{224,... | collective-permute-start | bytes 196616 | tf_op jit(solution)/shard_map/ppermute | solution.py:491
  70.8 6.3 %collective-permute-start.27 = (bf16[128,384]{1,0:T(8,128)(2,1)S(1)}, bf16[128,384]{1,0:T(8,128)(2,1)S(1)}, u32[]{:S(2)}, u32[]{:S(2)}) collective-permute-start(bf16[128,384]{1,0:T(8,128)(2,1)S(1)} %slice.4), channel_id=1, source_target_pairs={{0,192},{32,224},{64,0},{96,32},{128,64},{160,96},{192,128},{224,1... | collective-permute-start | bytes 294920 | tf_op jit(solution)/shard_map/ppermute | solution.py:492
  71.4 6.0 %collective-permute-start.24 = (bf16[128,256]{1,0:T(8,128)(2,1)S(1)}, bf16[128,256]{1,0:T(8,128)(2,1)S(1)}, u32[]{:S(2)}, u32[]{:S(2)}) collective-permute-start(bf16[128,256]{1,0:T(8,128)(2,1)S(1)} %piece_sum.1.refs_4_), channel_id=1, source_target_pairs={{0,64},{32,96},{64,128},{96,160},{128,192},{160,224},{192,0},{224,... | collective-permute-start | bytes 196616 | tf_op jit(solution)/shard_map/ppermute | solution.py:379
  74.2 6.0 %collective-permute-start.25 = (bf16[128,256]{1,0:T(8,128)(2,1)S(1)}, bf16[128,256]{1,0:T(8,128)(2,1)S(1)}, u32[]{:S(2)}, u32[]{:S(2)}) collective-permute-start(bf16[128,256]{1,0:T(8,128)(2,1)S(1)} %piece_sum.1.refs_4_), channel_id=1, source_target_pairs={{0,128},{32,160},{64,192},{96,224},{128,0},{160,32},{192,64},{224,... | collective-permute-start | bytes 196616 | tf_op jit(solution)/shard_map/ppermute | solution.py:379
  75.0 5.9 %collective-permute-start.26 = (bf16[128,256]{1,0:T(8,128)(2,1)S(1)}, bf16[128,256]{1,0:T(8,128)(2,1)S(1)}, u32[]{:S(2)}, u32[]{:S(2)}) collective-permute-start(bf16[128,256]{1,0:T(8,128)(2,1)S(1)} %piece_sum.1.refs_4_), channel_id=1, source_target_pairs={{0,192},{32,224},{64,0},{96,32},{128,64},{160,96},{192,128},{224,1... | collective-permute-start | bytes 196616 | tf_op jit(solution)/shard_map/ppermute | solution.py:379
  81.2 6.9 %collective-permute-start.28 = (bf16[640,128]{1,0:T(8,128)(2,1)S(1)}, bf16[640,128]{1,0:T(8,128)(2,1)S(1)}, u32[]{:S(2)}, u32[]{:S(2)}) collective-permute-start(bf16[640,128]{1,0:T(8,128)(2,1)S(1)} %get-tuple-element.55), channel_id=1, source_target_pairs={{0,32},{32,0},{64,96},{96,64},{128,160},{160,128},{192,224},{224,1... | collective-permute-start | bytes 491528 | tf_op jit(solution)/shard_map/ppermute | solution.py:513
  (6 other events, 10.0 us)
